TPU v7x, 256 devices: a whole 4x4x8 slice. The times are simulated.
256 devices in a mesh: tm: 16 (over z, core), chan: 16 (over x, y).
Axes of the slice: x: 4, y: 4, z: 8, core: 2. Of those that a mesh axis runs over, the one named last changes fastest.
Arguments:
- latent: bfloat16 [32, 1024, 16, 4], P('tm', 'chan'), may hold values from -81 to 81
- conv_first: bfloat16 [1024, 27, 1024], P('chan'), may hold values from -0.0390625 to 0.0390625
- conv_second: bfloat16 [1024, 27, 1024], P('chan'), may hold values from -0.0390625 to 0.0390625
- conv_upsample: bfloat16 [27, 1024, 4096], P(None, 'chan', 'tm'), may hold values from -0.0390625 to 0.0390625
Outputs:
- upsampled: bfloat16 [32, 512, 512], P('chan', 'tm')
All inputs are finite; a program needn't handle non-finite values.
Results may differ from a plain program's by a relative error of at most 0.0051.
Values may be sent and summed in bfloat16 or wider, within the bound.
No kernel may reach another device: no remote copies, remote signals or barrier semaphores. Data moves between devices by JAX's collectives and lax.ppermute only.
A program may use at most 128 MiB of HBM per device.

v0:
```python
import jax
import jax.numpy as jnp
from jax import lax
from jax.sharding import PartitionSpec as P

D = 1024


epsilon = 1e-06


def passed_along(value, axis, by):
    devices = lax.axis_size(axis)
    pairs = [(i, i + by) for i in range(devices) if 0 <= i + by < devices]
    return lax.ppermute(value, axis, pairs)


def with_halo(cells, sides, width):
    for axis, dim in sides:
        count = lax.axis_size(axis)
        ends = count - 1
        head = lax.slice_in_dim(cells, 0, width, axis=dim)
        tail = lax.slice_in_dim(cells, cells.shape[dim] - width, cells.shape[dim], axis=dim)
        cells = jnp.concatenate(
            [
                lax.ppermute(tail, axis, [(i, (i + 1) % count) for i in range(ends)]),
                cells,
                lax.ppermute(head, axis, [((i + 1) % count, i) for i in range(ends)]),
            ],
            axis=dim,
        )
    return cells


def tap_sum(padded, frames, rows, columns, weight_tap, form, shape_out):
    total = jnp.zeros(shape_out, jnp.float32)
    for frame_off in range(3):
        for row_off in range(3):
            for col_off in range(3):
                tap_index = 9 * frame_off + 3 * row_off + col_off
                tapped = padded[
                    frame_off : frame_off + frames,
                    :,
                    row_off : row_off + rows,
                    col_off : col_off + columns,
                ]
                total = total + jnp.einsum(
                    form, tapped, weight_tap(tap_index), preferred_element_type=jnp.float32
                )
    return total


def convolve(window, weight):
    frames = window.shape[0] - 2
    rows = window.shape[2]
    columns = window.shape[3]
    padded = jnp.pad(window, ((0, 0), (0, 0), (1, 1), (1, 1)))
    return tap_sum(
        padded,
        frames,
        rows,
        columns,
        lambda tap_index: weight[:, tap_index, :],
        "tchw,oc->tohw",
        (frames, weight.shape[0], rows, columns),
    )


def activate(window, squares):
    values = window.astype(jnp.float32)
    return jax.nn.silu(values * lax.rsqrt(squares / D + epsilon)).astype(jnp.bfloat16)


def causal_window(current):
    previous = passed_along(current, "tm", 1)
    repeated = jnp.concatenate([current[:1], current[:1]], 0)
    previous = jnp.where(lax.axis_index("tm") == 0, repeated, previous)
    return jnp.concatenate([previous, current], 0)


def block_conv(current, weight):
    window = causal_window(current)
    whole = lax.all_gather(window, "chan", axis=1, tiled=True)
    floats = whole.astype(jnp.float32)
    squares = jnp.sum(floats * floats, axis=1, keepdims=True)
    return convolve(activate(whole, squares), weight)


def depth_space(expanded):
    frames, channels, rows, columns = expanded.shape
    grouped = expanded.reshape(frames, channels // 8, 2, 2, 2, rows, columns)
    grouped = jnp.transpose(grouped, (5, 3, 1, 0, 2, 6, 4))
    return grouped.reshape(2 * rows, channels // 8, 4 * frames * columns)


def on_device(latent, conv_first, conv_second, conv_upsample):
    hidden = block_conv(latent, conv_first).astype(jnp.bfloat16)
    block_out = (latent.astype(jnp.float32) + block_conv(hidden, conv_second)).astype(jnp.bfloat16)
    all_frames = lax.all_gather(block_out, "tm", axis=0, tiled=True)
    frames = all_frames.shape[0]
    columns = all_frames.shape[3]
    rows_here = all_frames.shape[2] // lax.axis_size("chan")
    out_chan = conv_upsample.shape[2]
    bands = lax.all_to_all(all_frames, "chan", split_axis=2, concat_axis=1, tiled=True)
    framed = with_halo(bands, (("chan", 2),), 1)
    timed = jnp.concatenate([framed[:1], framed[:1], framed], 0)
    spatial = jnp.pad(timed, ((0, 0), (0, 0), (0, 0), (1, 1)))
    piece = lax.all_gather(conv_upsample, "chan", axis=1, tiled=True)
    expanded = tap_sum(
        spatial,
        frames,
        rows_here,
        columns,
        lambda tap_index: piece[tap_index],
        "tchw,co->tohw",
        (frames, out_chan, rows_here, columns),
    ).astype(jnp.bfloat16)
    return depth_space(expanded)


def solution(mesh):
    placed = (
        P("tm", "chan", None, None),
        P("chan", None, None),
        P("chan", None, None),
        P(None, "chan", "tm"),
    )
    return jax.shard_map(
        on_device, mesh=mesh, in_specs=placed, out_specs=P("chan", "tm", None), check_vma=False
    )
```

profile of v0, /device:TPU:1, one launch (start us, length us, event | category | flops | bytes accessed | tf_op | source)
XLA Modules:
  0.0 223.6 jit_solution(9982017920287073284)
XLA Ops:
  8.0 4.9 %collective-permute-start = (bf16[2,64,16,4]{1,2,3,0:T(8,128)(2,1)S(1)}, bf16[2,64,16,4]{1,2,3,0:T(8,128)(2,1)S(1)}, u32[]{:S(2)}, u32[]{:S(2)}) collective-permute-start(bf16[2,64,16,4]{1,2,3,0:T(8,128)(2,1)S(1)} %copy.25), channel_id=1, source_target_pairs={{0,16},{16,32},{32,48},{48,64},{64,80},{80,96},{96,112},{112,128},... | collective-permute-start | bytes 49160 | tf_op jit(solution)/shard_map/ppermute | solution.py:15
  14.3 48.0 %all_gather.12 = bf16[4,1024,16,4]{2,3,0,1:T(4,128)(2,1)} all-gather(bf16[4,64,16,4]{2,3,0,1:T(4,128)(2,1)S(1)} %copy.29), channel_id=1, replica_groups=mesh['tm'=16,'chan'=16] {'chan'}, dimensions={1}, use_global_device_ids=true | all-gather | bytes 557056 | tf_op jit(solution)/shard_map/all_gather | solution.py:83
  62.2 5.5 %copy.30 = bf16[4,1024,16,4]{1,2,3,0:T(8,128)(2,1)S(1)} copy(bf16[4,1024,16,4]{2,3,0,1:T(4,128)(2,1)} %all_gather.12) | data formatting | bytes 1048576 | tf_op jit(solution)/shard_map/all_gather | solution.py:83
  68.3 1.6 fusion.101
  77.6 5.5 %collective-permute-start.1 = (bf16[2,64,16,4]{1,2,3,0:T(8,128)(2,1)S(1)}, bf16[2,64,16,4]{1,2,3,0:T(8,128)(2,1)S(1)}, u32[]{:S(2)}, u32[]{:S(2)}) collective-permute-start(bf16[2,64,16,4]{1,2,3,0:T(8,128)(2,1)S(1)} %fusion.43), channel_id=1, source_target_pairs={{0,16},{16,32},{32,48},{48,64},{64,80},{80,96},{96,112},{112,128},... | collective-permute-start | bytes 49160 | tf_op jit(solution)/shard_map/ppermute | solution.py:15
  84.4 51.1 %all_gather.13 = bf16[4,1024,16,4]{2,3,0,1:T(4,128)(2,1)} all-gather(bf16[4,64,16,4]{2,3,0,1:T(4,128)(2,1)S(1)} %copy.31), channel_id=1, replica_groups=mesh['tm'=16,'chan'=16] {'chan'}, dimensions={1}, use_global_device_ids=true | all-gather | bytes 557056 | tf_op jit(solution)/shard_map/all_gather | solution.py:83
  135.5 5.5 %copy.32 = bf16[4,1024,16,4]{1,2,3,0:T(8,128)(2,1)S(1)} copy(bf16[4,1024,16,4]{2,3,0,1:T(4,128)(2,1)} %all_gather.13) | data formatting | bytes 1048576 | tf_op jit(solution)/shard_map/all_gather | solution.py:83
  141.6 1.4 fusion.102
  150.7 22.1 %all_gather.14 = bf16[32,64,16,4]{1,2,3,0:T(8,128)(2,1)S(1)} all-gather(bf16[2,64,16,4]{1,2,3,0:T(8,128)(2,1)S(1)} %fusion.44), channel_id=1, replica_groups=mesh['tm'=16,'chan'=16] {'tm'}, dimensions={0}, use_global_device_ids=true | all-gather | bytes 278528 | tf_op jit(solution)/shard_map/all_gather | solution.py:99
  173.5 12.2 %all_to_all.18 = bf16[16,2,4096]{2,1,0:T(2,128)(2,1)S(1)} all-to-all(bf16[16,2,4096]{2,1,0:T(2,128)(2,1)S(1)} %reshape.256), channel_id=1, replica_groups=mesh['tm'=16,'chan'=16] {'chan'}, dimensions={0} | all-to-all | bytes 524288 | tf_op jit(solution)/shard_map/all_to_all | solution.py:104
  187.0 2.1 collective-permute-start.2
  189.0 1.3 collective-permute-start.3
  190.7 2.3 %collective-permute-done.2 = bf16[32,1024,1,4]{1,0,3,2:T(8,128)(2,1)S(1)} collective-permute-done((bf16[32,1024,1,4]{1,0,3,2:T(8,128)(2,1)S(1)}, bf16[32,1024,1,4]{1,0,3,2:T(8,128)(2,1)S(1)}, u32[]{:S(2)}, u32[]{:S(2)}) %collective-permute-start.2) | collective-permute-done | bytes 262176 | tf_op jit(solution)/shard_map/ppermute | solution.py:26
  193.0 3.8 %collective-permute-done.3 = bf16[32,1024,1,4]{1,0,3,2:T(8,128)(2,1)S(1)} collective-permute-done((bf16[32,1024,1,4]{1,0,3,2:T(8,128)(2,1)S(1)}, bf16[32,1024,1,4]{1,0,3,2:T(8,128)(2,1)S(1)}, u32[]{:S(2)}, u32[]{:S(2)}) %collective-permute-start.3) | collective-permute-done | bytes 262176 | tf_op jit(solution)/shard_map/ppermute | solution.py:28
  197.3 1.4 fusion.55
  198.8 1.6 convolution_bitcast_fusion.2
  200.3 1.7 convolution_bitcast_fusion.3
  202.1 1.3 convolution_bitcast_fusion.5
  203.4 1.3 convolution_bitcast_fusion.6
  204.6 1.3 convolution_bitcast_fusion.8
  205.9 1.3 convolution_bitcast_fusion.9
  207.2 1.3 convolution_bitcast_fusion
  208.5 1.3 convolution_bitcast_fusion.1
  209.8 1.3 convolution_bitcast_fusion.7
  (112 shorter events, 28.5 us)
Async XLA Ops:
  6.5 190.8 %all-gather.2.cloned.1.call-start = ((), (), s32[]{:S(2)}) async-start(), calls=%async_computation.1 | async-start | bytes 15040512 | tf_op jit(solution)/shard_map/all_gather | solution.py:108
  8.0 5.9 %collective-permute-start = (bf16[2,64,16,4]{1,2,3,0:T(8,128)(2,1)S(1)}, bf16[2,64,16,4]{1,2,3,0:T(8,128)(2,1)S(1)}, u32[]{:S(2)}, u32[]{:S(2)}) collective-permute-start(bf16[2,64,16,4]{1,2,3,0:T(8,128)(2,1)S(1)} %copy.25), channel_id=1, source_target_pairs={{0,16},{16,32},{32,48},{48,64},{64,80},{80,96},{96,112},{112,128},... | collective-permute-start | bytes 49160 | tf_op jit(solution)/shard_map/ppermute | solution.py:15
  67.7 4.5 %copy-start.1 = (bf16[64,27,1024]{2,0,1:T(8,128)(2,1)S(1)}, bf16[64,27,1024]{2,0,1:T(8,128)(2,1)}, u32[]{:S(2)}) copy-start(bf16[64,27,1024]{2,0,1:T(8,128)(2,1)} %param.5) | copy-start | bytes 10616836
  77.6 6.5 %collective-permute-start.1 = (bf16[2,64,16,4]{1,2,3,0:T(8,128)(2,1)S(1)}, bf16[2,64,16,4]{1,2,3,0:T(8,128)(2,1)S(1)}, u32[]{:S(2)}, u32[]{:S(2)}) collective-permute-start(bf16[2,64,16,4]{1,2,3,0:T(8,128)(2,1)S(1)} %fusion.43), channel_id=1, source_target_pairs={{0,16},{16,32},{32,48},{48,64},{64,80},{80,96},{96,112},{112,128},... | collective-permute-start | bytes 49160 | tf_op jit(solution)/shard_map/ppermute | solution.py:15
  141.0 4.3 %copy-start.2 = (bf16[64,27,1024]{2,0,1:T(8,128)(2,1)S(1)}, bf16[64,27,1024]{2,0,1:T(8,128)(2,1)}, u32[]{:S(2)}) copy-start(bf16[64,27,1024]{2,0,1:T(8,128)(2,1)} %param.6) | copy-start | bytes 10616836
  148.5 2.0 copy-start.3
  187.0 6.0 %collective-permute-start.2 = (bf16[32,1024,1,4]{1,0,3,2:T(8,128)(2,1)S(1)}, bf16[32,1024,1,4]{1,0,3,2:T(8,128)(2,1)S(1)}, u32[]{:S(2)}, u32[]{:S(2)}) collective-permute-start(bf16[32,1024,1,4]{1,0,3,2:T(8,128)(2,1)S(1)} %all_to_all.16), channel_id=1, source_target_pairs={{0,1},{1,2},{2,3},{3,4},{4,5},{5,6},{6,7},{7,8},{8,9},{9,10},{10,1... | collective-permute-start | bytes 786440 | tf_op jit(solution)/shard_map/ppermute | solution.py:26
  189.0 7.8 %collective-permute-start.3 = (bf16[32,1024,1,4]{1,0,3,2:T(8,128)(2,1)S(1)}, bf16[32,1024,1,4]{1,0,3,2:T(8,128)(2,1)S(1)}, u32[]{:S(2)}, u32[]{:S(2)}) collective-permute-start(bf16[32,1024,1,4]{1,0,3,2:T(8,128)(2,1)S(1)} %all_to_all.16), channel_id=1, source_target_pairs={{1,0},{2,1},{3,2},{4,3},{5,4},{6,5},{7,6},{8,7},{9,8},{10,9},{11,1... | collective-permute-start | bytes 786440 | tf_op jit(solution)/shard_map/ppermute | solution.py:28
  197.3 13.7 %copy-start = (bf16[27,1024,256]{2,1,0:T(8,128)(2,1)S(1)}, bf16[27,1024,256]{2,1,0:T(8,128)(2,1)}, u32[]{:S(2)}) copy-start(bf16[27,1024,256]{2,1,0:T(8,128)(2,1)} %all-gather.2.cloned.1.call-done) | copy-start | bytes 42467332
Sparse Core Ops, SparseCore 0:
  9.8 140.5 all-gather.1
where the time goes:
time: 227 us; the launch traced here: 224 us
  blocking collectives  133 us (59%)
  matrix products  35.8 us (16%)
  local copies, waits for them, and re-layouts  16 us (7%)
  between operations  14.2 us (6%)
  starting transfers between devices  13.8 us (6%)
  waiting for transfers between devices  8.8 us (4%)
    all_gather x2, blocking collectives, block_conv(): whole = lax.all_gather(window, 'chan', axis=1, tiled=True)  99.1 us
    dot_general x81, matrix products, tap_sum(): jnp.einsum(form, tapped, weight_tap(tap_index), preferred_element_type=jn...  35.8 us
    all_gather x1, blocking collectives, on_device(): all_frames = lax.all_gather(block_out, 'tm', axis=0, tiled=True)  22.1 us
    all_to_all x1, blocking collectives, on_device(): lax.all_to_all(all_frames, 'chan', split_axis=2, concat_axis=1, tiled=True)  12.2 us
    all_gather x2, local copies, waits for them, and re-layouts, block_conv(): whole = lax.all_gather(window, 'chan', axis=1, tiled=True)  11 us
    ppermute x2, starting transfers between devices, passed_along(): return lax.ppermute(value, axis, pairs)  10.4 us
  transfers between devices with their start and end apart: 5, of which 4 were waited for; matrix products, arithmetic and copies ran while one was open for 15% of the time, Pallas kernels for 0%

commit v1 on v0

v1 whole, which is shorter than its diff:
```python
import functools

import jax
import jax.numpy as jnp
from jax import lax
from jax.experimental import pallas as pl
from jax.experimental.pallas import tpu as pltpu
from jax.sharding import PartitionSpec as P

EPSILON = 1e-06
F32 = jnp.float32
BF16 = jnp.bfloat16
COLS = 4
FRAMES = 2
CELL = FRAMES * COLS
LANES = 128
ROWS = 16
MIB = 1 << 20


def lane_ids():
    lane = lax.broadcasted_iota(jnp.int32, (1, LANES), 1)
    return lane // CELL, (lane // COLS) % FRAMES, lane % COLS


def spatial_sum(product, first_tap, outs):
    row, _, col = lane_ids()
    total = None
    for row_off in range(3):
        part = None
        for col_off in range(3):
            start = (first_tap + 3 * row_off + col_off) * outs
            piece = product[start : start + outs]
            if col_off == 0:
                piece = jnp.where(col >= 1, pltpu.roll(piece, 1, 1), 0.0)
            if col_off == 2:
                piece = jnp.where(col < COLS - 1, pltpu.roll(piece, LANES - 1, 1), 0.0)
            part = piece if part is None else part + piece
        if row_off == 0:
            part = jnp.where(row >= 1, pltpu.roll(part, CELL, 1), 0.0)
        if row_off == 2:
            part = jnp.where(row < ROWS - 1, pltpu.roll(part, LANES - CELL, 1), 0.0)
        total = part if total is None else total + part
    return total


def block_kernel(whole_ref, weight_ref, own_ref, later_ref):
    depth = whole_ref.shape[0]
    outs = own_ref.shape[0]
    values = whole_ref[...].astype(F32)
    squares = jnp.sum(values * values, axis=0, keepdims=True)
    scaled = values * lax.rsqrt(squares / depth + EPSILON)
    act = (scaled / (1.0 + jnp.exp(-scaled))).astype(BF16)
    product = jnp.dot(weight_ref[...], act, preferred_element_type=F32)
    frame = lane_ids()[1]
    oldest = spatial_sum(product, 0, outs)
    middle = spatial_sum(product, 9, outs)
    newest = spatial_sum(product, 18, outs)
    first = lax.axis_index("tm") == 0
    start = jnp.where(frame == 0, middle + oldest, pltpu.roll(oldest, COLS, 1))
    own = newest + jnp.where(frame == 1, pltpu.roll(middle, COLS, 1), 0.0)
    own_ref[...] = own + jnp.where(first, start, 0.0)
    later_ref[...] = oldest + jnp.where(frame == 0, pltpu.roll(middle, LANES - COLS, 1), 0.0)


def block_conv(whole, weight, outs):
    shape = jax.ShapeDtypeStruct((outs, LANES), F32)
    own, later = pl.pallas_call(
        block_kernel,
        out_shape=(shape, shape),
        compiler_params=pltpu.CompilerParams(vmem_limit_bytes=40 * MIB),
    )(whole, weight)
    devices = lax.axis_size("tm")
    earlier = lax.ppermute(later, "tm", [(i, i + 1) for i in range(devices - 1)])
    return own + earlier


def gathered(value, axis):
    copies = jnp.broadcast_to(value, (lax.axis_size(axis),) + value.shape)
    return lax.all_to_all(copies, axis, 0, 0, tiled=True)


def upsample_kernel(all_ref, weight_ref, out_ref, shifted):
    count, depth, _ = all_ref.shape
    lane = lax.broadcasted_iota(jnp.int32, (1, LANES), 1)
    col = lane % COLS
    blocks = [all_ref[i].astype(F32) for i in range(count)]
    bit = 1
    while bit < count:
        step = bit * CELL
        upper = (lane // step) % 2 == 1
        swapped = list(blocks)
        for i in range(count):
            if i & bit == 0:
                low, high = blocks[i], blocks[i | bit]
                swapped[i] = jnp.where(upper, pltpu.roll(high, step, 1), low)
                swapped[i | bit] = jnp.where(upper, high, pltpu.roll(low, LANES - step, 1))
        blocks = swapped
        bit *= 2
    zero = jnp.zeros((depth, LANES), BF16)
    for k in range(9):
        shifted[k, 0] = zero
        shifted[k, count + 1] = zero
    for r in range(count):
        value = blocks[r]
        back = jnp.where(lane < COLS, value, pltpu.roll(value, COLS, 1))
        back_two = jnp.where(lane < COLS, value, pltpu.roll(back, COLS, 1))
        for frame_off, moved in enumerate((back_two, back, value)):
            left = jnp.where(col >= 1, pltpu.roll(moved, 1, 1), 0.0)
            right = jnp.where(col < COLS - 1, pltpu.roll(moved, LANES - 1, 1), 0.0)
            shifted[3 * frame_off, r + 1] = left.astype(BF16)
            shifted[3 * frame_off + 1, r + 1] = moved.astype(BF16)
            shifted[3 * frame_off + 2, r + 1] = right.astype(BF16)
    pair = 2
    for r in range(0, count, pair):
        columns = []
        for j in range(pair):
            columns.append(
                jnp.concatenate(
                    [
                        shifted[3 * kt + ks, r + j + kr]
                        for kt in range(3)
                        for kr in range(3)
                        for ks in range(3)
                    ],
                    axis=0,
                )
            )
        spread = jnp.concatenate(columns, axis=1)
        result = lax.dot_general(
            weight_ref[...], spread, (((0,), (0,)), ((), ())), preferred_element_type=F32
        ).astype(BF16)
        for j in range(pair):
            out_ref[r + j] = result[:, j * LANES : (j + 1) * LANES]


def finish_kernel(parts_ref, out_ref, total_ref):
    count = parts_ref.shape[0]
    channels = out_ref.shape[1]
    total = parts_ref[0].astype(F32)
    for i in range(1, count):
        total = total + parts_ref[i].astype(F32)
    total_ref[...] = total
    wide = out_ref.shape[2]
    source = lax.broadcasted_iota(jnp.int32, (LANES, wide), 0)
    target = lax.broadcasted_iota(jnp.int32, (LANES, wide), 1)
    base = (source // COLS) * (4 * COLS) + (source % COLS) * 2
    for p2 in range(2):
        result = jnp.zeros((channels, wide), F32)
        for p1 in range(2):
            for p3 in range(2):
                rows = total_ref[pl.ds(4 * p1 + 2 * p2 + p3, channels, stride=8), :]
                place = jnp.where(target == base + 2 * COLS * p1 + p3, 1.0, 0.0).astype(BF16)
                result = result + jnp.dot(rows.astype(BF16), place, preferred_element_type=F32)
        out_ref[p2] = result.astype(BF16)


def on_device(latent, conv_first, conv_second, conv_upsample):
    channels = latent.shape[1]
    places = jnp.transpose(latent, (1, 2, 0, 3)).reshape(channels, LANES)

    def taps(weight):
        outs, count, depth = weight.shape
        return jnp.transpose(weight, (1, 0, 2)).reshape(count * outs, depth)

    whole = gathered(places, "chan").reshape(-1, LANES)
    hidden = block_conv(whole, taps(conv_first), channels).astype(BF16)
    whole = gathered(hidden, "chan").reshape(-1, LANES)
    block = block_conv(whole, taps(conv_second), channels)
    block_out = (places.astype(F32) + block).astype(BF16)
    frames = gathered(block_out, "tm")
    count = frames.shape[0]
    outs = conv_upsample.shape[2]
    partial = pl.pallas_call(
        upsample_kernel,
        out_shape=jax.ShapeDtypeStruct((count, outs, LANES), BF16),
        scratch_shapes=[pltpu.VMEM((9, count + 2, channels, LANES), BF16)],
        compiler_params=pltpu.CompilerParams(vmem_limit_bytes=40 * MIB),
    )(frames, conv_upsample.reshape(-1, outs))
    parts = lax.all_to_all(partial, "chan", 0, 0, tiled=True)
    return pl.pallas_call(
        finish_kernel,
        out_shape=jax.ShapeDtypeStruct((2, outs // 8, 4 * LANES), BF16),
        scratch_shapes=[pltpu.VMEM((outs, LANES), F32)],
        compiler_params=pltpu.CompilerParams(vmem_limit_bytes=40 * MIB),
    )(parts)


def solution(mesh):
    placed = (
        P("tm", "chan", None, None),
        P("chan", None, None),
        P("chan", None, None),
        P(None, "chan", "tm"),
    )
    return jax.shard_map(
        on_device, mesh=mesh, in_specs=placed, out_specs=P("chan", "tm", None), check_vma=False
    )
```

time: 227 us -> 94.3 us (0.42); the launches traced: 224 us -> 93.9 us
  blocking collectives: 133 us -> 68.8 us
  matrix products: 35.8 us -> 0 us
  between operations: 14.2 us -> 0.09 us
  local copies, waits for them, and re-layouts: 16 us -> 3.01 us
  Pallas kernels: 0 us -> 8.73 us
  waiting for transfers between devices: 8.8 us -> 2 us
  starting transfers between devices: 13.8 us -> 11.2 us
    all_gather x3 -> x0, blocking collectives: 121 us -> none  [the longest x2 99.1 us: block_conv(): whole = lax.all_gather(window, 'chan', axis=1, tiled=True)]
    all_to_all x1 -> x4, blocking collectives: 12.2 us -> 68.8 us  [the longest x3 48.5 us: gathered(): return lax.all_to_all(copies, axis, 0, 0, tiled=True)]
    dot_general x81 -> x0, matrix products: 35.8 us -> none  [tap_sum(): jnp.einsum(form, tapped, weight_tap(tap_index), preferred_element_type=jn...]
    all_gather x3 -> x0, local copies, waits for them, and re-layouts: 11.2 us -> none  [the longest x2 11 us: block_conv(): whole = lax.all_gather(window, 'chan', axis=1, tiled=True)]
    pallas_call x0 -> x4, Pallas kernels: none -> 8.73 us  [the longest x1 4.72 us: on_device(): pl.pallas_call(upsample_kernel, out_shape=jax.ShapeDtypeStruct((count, ou...]
    ppermute x4 -> x2, waiting for transfers between devices: 8.07 us -> 2 us  [block_conv(): lax.ppermute(later, 'tm', [(i, i + 1) for i in range(devices - 1)])]
    ppermute x4 -> x2, starting transfers between devices: 13.8 us -> 11.2 us  [block_conv(): lax.ppermute(later, 'tm', [(i, i + 1) for i in range(devices - 1)])]
  transfers between devices with their start and end apart: 5 -> 2, of which waited for: 4 -> 2; matrix products, arithmetic and copies ran while one was open for 15% -> 0% of each run, Pallas kernels for 0% -> 0%
where the time goes in v1:
time: 94.3 us; the launch traced here: 93.9 us
  blocking collectives  68.8 us (73%)
  starting transfers between devices  11.2 us (12%)
  Pallas kernels  8.73 us (9%)
  local copies, waits for them, and re-layouts  3.01 us (3%)
  waiting for transfers between devices  2 us (2%)
    all_to_all x3, blocking collectives, gathered(): return lax.all_to_all(copies, axis, 0, 0, tiled=True)  48.5 us
    all_to_all x1, blocking collectives, on_device(): parts = lax.all_to_all(partial, 'chan', 0, 0, tiled=True)  20.3 us
    ppermute x2, starting transfers between devices, block_conv(): lax.ppermute(later, 'tm', [(i, i + 1) for i in range(devices - 1)])  11.2 us
    pallas_call x1, Pallas kernels, on_device(): pl.pallas_call(upsample_kernel, out_shape=jax.ShapeDtypeStruct((count, ou...  4.72 us
    pallas_call x2, Pallas kernels, block_conv(): pl.pallas_call(block_kernel, out_shape=(shape, shape), compiler_params=pl...  2.85 us
    unnamed x6, local copies, waits for them, and re-layouts  2.01 us
    ppermute x2, waiting for transfers between devices, block_conv(): lax.ppermute(later, 'tm', [(i, i + 1) for i in range(devices - 1)])  2 us
  transfers between devices with their start and end apart: 2, of which 2 were waited for; matrix products, arithmetic and copies ran while one was open for 0% of the time, Pallas kernels for 0%

profile of v1, /device:TPU:1, one launch (start us, length us, event | category | flops | bytes accessed | tf_op | source)
XLA Modules:
  0.0 93.9 jit_solution(6906886618969662888)
XLA Ops:
  0.0 0.8 copy.6
  0.8 0.1 copy.7
  0.9 0.1 broadcast_in_dim.9
  0.9 14.8 %all_to_all.20 = bf16[16,64,128]{2,1,0:T(8,128)(2,1)S(1)} all-to-all(bf16[16,64,128]{2,1,0:T(8,128)(2,1)S(1)} %broadcast_in_dim.9), channel_id=1, replica_groups=mesh['tm'=16,'chan'=16] {'chan'}, dimensions={0} | all-to-all | bytes 524288 | tf_op jit(solution)/shard_map/all_to_all | solution.py:80
  15.8 0.0 copy-start
  15.8 2.0 %copy-done = bf16[64,27,1024]{2,0,1:T(8,128)(2,1)S(1)} copy-done((bf16[64,27,1024]{2,0,1:T(8,128)(2,1)S(1)}, bf16[64,27,1024]{2,0,1:T(8,128)(2,1)}, u32[]{:S(2)}) %copy-start) | copy-done | bytes 3538968
  17.8 0.0 copy-start.1
  17.8 1.4 %shard_map.46 = (f32[64,128]{1,0:T(8,128)S(1)}, f32[64,128]{1,0:T(8,128)S(1)}) custom-call(bf16[1024,128]{1,0:T(8,128)(2,1)S(1)} %bitcast.13, bf16[1728,1024]{1,0:T(8,128)(2,1)S(1)} %bitcast.11), custom_call_target="tpu_custom_call" | custom-call | tf_op jit(solution)/shard_map/pallas_call | solution.py:68
  19.2 0.0 copy-start.2
  19.2 5.6 %collective-permute-start = (f32[64,128]{1,0:T(8,128)S(1)}, f32[64,128]{1,0:T(8,128)S(1)}, u32[]{:S(2)}, u32[]{:S(2)}) collective-permute-start(f32[64,128]{1,0:T(8,128)S(1)} %get-tuple-element.10), channel_id=1, source_target_pairs={{0,16},{16,32},{32,48},{48,64},{64,80},{80,96},{96,112},{112,128},... | collective-permute-start | bytes 98312 | tf_op jit(solution)/shard_map/ppermute | solution.py:74
  24.8 1.0 %collective-permute-done = f32[64,128]{1,0:T(8,128)S(1)} collective-permute-done((f32[64,128]{1,0:T(8,128)S(1)}, f32[64,128]{1,0:T(8,128)S(1)}, u32[]{:S(2)}, u32[]{:S(2)}) %collective-permute-start) | collective-permute-done | bytes 32800 | tf_op jit(solution)/shard_map/ppermute | solution.py:74
  25.9 10.5 %all_to_all.21 = bf16[16,64,128]{2,1,0:T(8,128)(2,1)S(1)} all-to-all(bf16[16,64,128]{2,1,0:T(8,128)(2,1)S(1)} %broadcast_in_dim.10), channel_id=1, replica_groups=mesh['tm'=16,'chan'=16] {'chan'}, dimensions={0} | all-to-all | bytes 524288 | tf_op jit(solution)/shard_map/all_to_all | solution.py:80
  36.4 0.0 copy-done.1
  36.4 1.4 %shard_map.47 = (f32[64,128]{1,0:T(8,128)S(1)}, f32[64,128]{1,0:T(8,128)S(1)}) custom-call(bf16[1024,128]{1,0:T(8,128)(2,1)S(1)} %bitcast.14, bf16[1728,1024]{1,0:T(8,128)(2,1)S(1)} %bitcast.12), custom_call_target="tpu_custom_call" | custom-call | tf_op jit(solution)/shard_map/pallas_call | solution.py:68
  37.8 5.7 %collective-permute-start.1 = (f32[64,128]{1,0:T(8,128)S(1)}, f32[64,128]{1,0:T(8,128)S(1)}, u32[]{:S(2)}, u32[]{:S(2)}) collective-permute-start(f32[64,128]{1,0:T(8,128)S(1)} %get-tuple-element.12), channel_id=1, source_target_pairs={{0,16},{16,32},{32,48},{48,64},{64,80},{80,96},{96,112},{112,128},... | collective-permute-start | bytes 98312 | tf_op jit(solution)/shard_map/ppermute | solution.py:74
  43.5 1.0 %collective-permute-done.1 = f32[64,128]{1,0:T(8,128)S(1)} collective-permute-done((f32[64,128]{1,0:T(8,128)S(1)}, f32[64,128]{1,0:T(8,128)S(1)}, u32[]{:S(2)}, u32[]{:S(2)}) %collective-permute-start.1) | collective-permute-done | bytes 32800 | tf_op jit(solution)/shard_map/ppermute | solution.py:74
  44.5 23.1 %all_to_all.22.all_ref = bf16[16,64,128]{2,1,0:T(8,128)(2,1)S(1)} all-to-all(bf16[16,64,128]{2,1,0:T(8,128)(2,1)S(1)} %broadcast_in_dim.11), channel_id=1, replica_groups=mesh['tm'=16,'chan'=16] {'tm'}, dimensions={0} | all-to-all | bytes 524288 | tf_op jit(solution)/shard_map/all_to_all | solution.py:80
  67.7 0.0 copy-done.2
  67.7 4.7 %shard_map.48 = bf16[16,256,128]{2,1,0:T(8,128)(2,1)S(1)} custom-call(bf16[16,64,128]{2,1,0:T(8,128)(2,1)S(1)} %all_to_all.22.all_ref, bf16[1728,256]{1,0:T(8,128)(2,1)S(1)} %bitcast.15), custom_call_target="tpu_custom_call" | custom-call | tf_op jit(solution)/shard_map/pallas_call | solution.py:174
  72.4 20.3 %all_to_all.23.parts_ref = bf16[16,256,128]{2,1,0:T(8,128)(2,1)S(1)} all-to-all(bf16[16,256,128]{2,1,0:T(8,128)(2,1)S(1)} %shard_map.48), channel_id=1, replica_groups=mesh['tm'=16,'chan'=16] {'chan'}, dimensions={0} | all-to-all | bytes 2097152 | tf_op jit(solution)/shard_map/all_to_all | solution.py:180
  92.8 1.2 %shard_map.49 = bf16[2,32,512]{2,1,0:T(8,128)(2,1)} custom-call(bf16[16,256,128]{2,1,0:T(8,128)(2,1)S(1)} %all_to_all.23.parts_ref), custom_call_target="tpu_custom_call" | custom-call | tf_op jit(solution)/shard_map/pallas_call | solution.py:181
  (4 shorter events, 0.1 us)
Async XLA Ops:
  15.8 2.0 %copy-start = (bf16[64,27,1024]{2,0,1:T(8,128)(2,1)S(1)}, bf16[64,27,1024]{2,0,1:T(8,128)(2,1)}, u32[]{:S(2)}) copy-start(bf16[64,27,1024]{2,0,1:T(8,128)(2,1)} %param.5) | copy-start | bytes 10616836
  17.8 18.6 %copy-start.1 = (bf16[64,27,1024]{2,0,1:T(8,128)(2,1)S(1)}, bf16[64,27,1024]{2,0,1:T(8,128)(2,1)}, u32[]{:S(2)}) copy-start(bf16[64,27,1024]{2,0,1:T(8,128)(2,1)} %param.6) | copy-start | bytes 10616836
  19.2 48.5 %copy-start.2 = (bf16[27,64,256]{2,1,0:T(8,128)(2,1)S(1)}, bf16[27,64,256]{2,1,0:T(8,128)(2,1)}, u32[]{:S(2)}) copy-start(bf16[27,64,256]{2,1,0:T(8,128)(2,1)} %param.7) | copy-start | bytes 2654212
  19.2 6.6 %collective-permute-start = (f32[64,128]{1,0:T(8,128)S(1)}, f32[64,128]{1,0:T(8,128)S(1)}, u32[]{:S(2)}, u32[]{:S(2)}) collective-permute-start(f32[64,128]{1,0:T(8,128)S(1)} %get-tuple-element.10), channel_id=1, source_target_pairs={{0,16},{16,32},{32,48},{48,64},{64,80},{80,96},{96,112},{112,128},... | collective-permute-start | bytes 98312 | tf_op jit(solution)/shard_map/ppermute | solution.py:74
  37.8 6.7 %collective-permute-start.1 = (f32[64,128]{1,0:T(8,128)S(1)}, f32[64,128]{1,0:T(8,128)S(1)}, u32[]{:S(2)}, u32[]{:S(2)}) collective-permute-start(f32[64,128]{1,0:T(8,128)S(1)} %get-tuple-element.12), channel_id=1, source_target_pairs={{0,16},{16,32},{32,48},{48,64},{64,80},{80,96},{96,112},{112,128},... | collective-permute-start | bytes 98312 | tf_op jit(solution)/shard_map/ppermute | solution.py:74

commit v2 on v1

--- a/solution.py
+++ b/solution.py
@@ -44,6 +44,14 @@
     return total
 
 
+def start_kernel(latent_ref, places_ref, copies_ref):
+    cells = [latent_ref[t, r] for r in range(ROWS) for t in range(FRAMES)]
+    places = jnp.concatenate(cells, axis=0).astype(F32).T.astype(BF16)
+    places_ref[...] = places
+    for i in range(copies_ref.shape[0]):
+        copies_ref[i] = places
+
+
 def block_kernel(whole_ref, weight_ref, own_ref, later_ref):
     depth = whole_ref.shape[0]
     outs = own_ref.shape[0]
@@ -68,15 +76,32 @@
     own, later = pl.pallas_call(
         block_kernel,
         out_shape=(shape, shape),
-        compiler_params=pltpu.CompilerParams(vmem_limit_bytes=40 * MIB),
+        compiler_params=pltpu.CompilerParams(vmem_limit_bytes=16 * MIB),
+        cost_estimate=pl.CostEstimate(flops=4 * 10**9, bytes_accessed=8 * MIB, transcendentals=0),
     )(whole, weight)
     devices = lax.axis_size("tm")
-    earlier = lax.ppermute(later, "tm", [(i, i + 1) for i in range(devices - 1)])
-    return own + earlier
-
-
-def gathered(value, axis):
-    copies = jnp.broadcast_to(value, (lax.axis_size(axis),) + value.shape)
+    earlier = lax.ppermute(later, "tm", [(i, (i + 1) % devices) for i in range(devices)])
+    return own, earlier
+
+
+def join_kernel(own_ref, earlier_ref, *rest):
+    copies_ref = rest[-1]
+    value = own_ref[...] + jnp.where(lax.axis_index("tm") == 0, 0.0, earlier_ref[...])
+    for ref in rest[:-1]:
+        value = ref[...].astype(F32) + value
+    value = value.astype(BF16)
+    for i in range(copies_ref.shape[0]):
+        copies_ref[i] = value
+
+
+def joined(parts, axis):
+    shape = (lax.axis_size(axis),) + parts[0].shape
+    copies = pl.pallas_call(
+        join_kernel,
+        out_shape=jax.ShapeDtypeStruct(shape, BF16),
+        compiler_params=pltpu.CompilerParams(vmem_limit_bytes=8 * MIB),
+        cost_estimate=pl.CostEstimate(flops=8 * 10**9, bytes_accessed=MIB, transcendentals=0),
+    )(*parts)
     return lax.all_to_all(copies, axis, 0, 0, tiled=True)
 
 
@@ -157,32 +182,40 @@
 
 def on_device(latent, conv_first, conv_second, conv_upsample):
     channels = latent.shape[1]
-    places = jnp.transpose(latent, (1, 2, 0, 3)).reshape(channels, LANES)
+    shape = (channels, LANES)
+    places, copies = pl.pallas_call(
+        start_kernel,
+        out_shape=(
+            jax.ShapeDtypeStruct(shape, BF16),
+            jax.ShapeDtypeStruct((lax.axis_size("chan"),) + shape, BF16),
+        ),
+        compiler_params=pltpu.CompilerParams(vmem_limit_bytes=8 * MIB),
+        cost_estimate=pl.CostEstimate(flops=8 * 10**9, bytes_accessed=MIB, transcendentals=0),
+    )(jnp.transpose(latent, (0, 2, 3, 1)))
 
     def taps(weight):
         outs, count, depth = weight.shape
         return jnp.transpose(weight, (1, 0, 2)).reshape(count * outs, depth)
 
-    whole = gathered(places, "chan").reshape(-1, LANES)
-    hidden = block_conv(whole, taps(conv_first), channels).astype(BF16)
-    whole = gathered(hidden, "chan").reshape(-1, LANES)
-    block = block_conv(whole, taps(conv_second), channels)
-    block_out = (places.astype(F32) + block).astype(BF16)
-    frames = gathered(block_out, "tm")
+    whole = lax.all_to_all(copies, "chan", 0, 0, tiled=True).reshape(-1, LANES)
+    parts = block_conv(whole, taps(conv_first), channels)
+    whole = joined(parts, "chan").reshape(-1, LANES)
+    parts = block_conv(whole, taps(conv_second), channels)
+    frames = joined((*parts, places), "tm")
     count = frames.shape[0]
     outs = conv_upsample.shape[2]
     partial = pl.pallas_call(
         upsample_kernel,
         out_shape=jax.ShapeDtypeStruct((count, outs, LANES), BF16),
         scratch_shapes=[pltpu.VMEM((9, count + 2, channels, LANES), BF16)],
-        compiler_params=pltpu.CompilerParams(vmem_limit_bytes=40 * MIB),
+        compiler_params=pltpu.CompilerParams(vmem_limit_bytes=16 * MIB),
     )(frames, conv_upsample.reshape(-1, outs))
     parts = lax.all_to_all(partial, "chan", 0, 0, tiled=True)
     return pl.pallas_call(
         finish_kernel,
         out_shape=jax.ShapeDtypeStruct((2, outs // 8, 4 * LANES), BF16),
         scratch_shapes=[pltpu.VMEM((outs, LANES), F32)],
-        compiler_params=pltpu.CompilerParams(vmem_limit_bytes=40 * MIB),
+        compiler_params=pltpu.CompilerParams(vmem_limit_bytes=16 * MIB),
     )(parts)
 
 

time: 94.3 us -> 88.8 us (0.942)
  starting transfers between devices: 11.2 us -> 7.35 us
  local copies, waits for them, and re-layouts: 3.01 us -> 0.77 us
    ppermute x2, starting transfers between devices: 11.2 us -> 7.35 us  [block_conv(): lax.ppermute(later, 'tm', [(i, (i + 1) % devices) for i in range(devices)])]
    unnamed x6 -> x8, local copies, waits for them, and re-layouts: 2.01 us -> 0.77 us
where the time goes in v2:
time: 88.8 us; the launch traced here: 88.5 us
  blocking collectives  68.9 us (78%)
  Pallas kernels  8.87 us (10%)
  starting transfers between devices  7.35 us (8%)
  waiting for transfers between devices  2.58 us (3%)
    all_to_all x2, blocking collectives, joined(): return lax.all_to_all(copies, axis, 0, 0, tiled=True)  33.5 us
    all_to_all x1, blocking collectives, on_device(): parts = lax.all_to_all(partial, 'chan', 0, 0, tiled=True)  20.3 us
    all_to_all x1, blocking collectives, on_device(): whole = lax.all_to_all(copies, 'chan', 0, 0, tiled=True).reshape(-1, LANES)  15.1 us
    ppermute x2, starting transfers between devices, block_conv(): lax.ppermute(later, 'tm', [(i, (i + 1) % devices) for i in range(devices)])  7.35 us
    pallas_call x1, Pallas kernels, on_device(): pl.pallas_call(upsample_kernel, out_shape=jax.ShapeDtypeStruct((count, ou...  4.72 us
    pallas_call x2, Pallas kernels, block_conv(): pl.pallas_call(block_kernel, out_shape=(shape, shape), compiler_params=pl...  2.85 us
    ppermute x2, waiting for transfers between devices, block_conv(): lax.ppermute(later, 'tm', [(i, (i + 1) % devices) for i in range(devices)])  2.58 us
  transfers between devices with their start and end apart: 2, of which 2 were waited for; matrix products, arithmetic and copies ran while one was open for 0% of the time, Pallas kernels for 0%

profile of v2, /device:TPU:1, one launch (start us, length us, event | category | flops | bytes accessed | tf_op | source)
XLA Modules:
  0.0 88.5 jit_solution(6636054998941204328)
XLA Ops:
  0.0 0.0 copy-start.3
  0.0 0.8 copy-done.3
  0.8 0.0 copy-start.1
  0.8 0.1 shard_map.46
  0.9 15.1 %all_to_all.20 = bf16[16,64,128]{2,1,0:T(8,128)(2,1)S(1)} all-to-all(bf16[16,64,128]{2,1,0:T(8,128)(2,1)S(1)} %get-tuple-element.11), channel_id=1, replica_groups=mesh['tm'=16,'chan'=16] {'chan'}, dimensions={0} | all-to-all | bytes 524288 | tf_op jit(solution)/shard_map/all_to_all | solution.py:200
  16.0 0.0 copy-done.1
  16.0 1.4 %shard_map.47 = (f32[64,128]{1,0:T(8,128)S(1)}, f32[64,128]{1,0:T(8,128)S(1)}) custom-call(bf16[1024,128]{1,0:T(8,128)(2,1)S(1)} %bitcast.11, bf16[1728,1024]{1,0:T(8,128)(2,1)S(1)} %bitcast.13), custom_call_target="tpu_custom_call" | custom-call | flops 4000000000 | bytes 8388608 | tf_op jit(solution)/shard_map/pallas_call | solution.py:76
  17.4 3.5 %collective-permute-start = (f32[64,128]{1,0:T(8,128)S(1)}, f32[64,128]{1,0:T(8,128)S(1)}, u32[]{:S(2)}, u32[]{:S(2)}) collective-permute-start(f32[64,128]{1,0:T(8,128)S(1)} %get-tuple-element.13), channel_id=1, source_target_pairs={{0,16},{16,32},{32,48},{48,64},{64,80},{80,96},{96,112},{112,128},... | collective-permute-start | bytes 98312 | tf_op jit(solution)/shard_map/ppermute | solution.py:83
  21.0 1.0 %collective-permute-done.earlier_ref = f32[64,128]{1,0:T(8,128)S(1)} collective-permute-done((f32[64,128]{1,0:T(8,128)S(1)}, f32[64,128]{1,0:T(8,128)S(1)}, u32[]{:S(2)}, u32[]{:S(2)}) %collective-permute-start) | collective-permute-done | bytes 32800 | tf_op jit(solution)/shard_map/ppermute | solution.py:83
  22.0 0.0 copy-start.2
  22.0 10.7 %all_to_all.21 = bf16[16,64,128]{2,1,0:T(8,128)(2,1)S(1)} all-to-all(bf16[16,64,128]{2,1,0:T(8,128)(2,1)S(1)} %shard_map.48), channel_id=1, replica_groups=mesh['tm'=16,'chan'=16] {'chan'}, dimensions={0} | all-to-all | bytes 524288 | tf_op jit(solution)/shard_map/all_to_all | solution.py:105
  32.7 0.0 copy-done.2
  32.7 1.4 %shard_map.49 = (f32[64,128]{1,0:T(8,128)S(1)}, f32[64,128]{1,0:T(8,128)S(1)}) custom-call(bf16[1024,128]{1,0:T(8,128)(2,1)S(1)} %bitcast.12, bf16[1728,1024]{1,0:T(8,128)(2,1)S(1)} %bitcast.14), custom_call_target="tpu_custom_call" | custom-call | flops 4000000000 | bytes 8388608 | tf_op jit(solution)/shard_map/pallas_call | solution.py:76
  34.2 3.8 %collective-permute-start.1 = (f32[64,128]{1,0:T(8,128)S(1)}, f32[64,128]{1,0:T(8,128)S(1)}, u32[]{:S(2)}, u32[]{:S(2)}) collective-permute-start(f32[64,128]{1,0:T(8,128)S(1)} %get-tuple-element.15), channel_id=1, source_target_pairs={{0,16},{16,32},{32,48},{48,64},{64,80},{80,96},{96,112},{112,128},... | collective-permute-start | bytes 98312 | tf_op jit(solution)/shard_map/ppermute | solution.py:83
  38.0 1.6 %collective-permute-done.1.earlier_ref = f32[64,128]{1,0:T(8,128)S(1)} collective-permute-done((f32[64,128]{1,0:T(8,128)S(1)}, f32[64,128]{1,0:T(8,128)S(1)}, u32[]{:S(2)}, u32[]{:S(2)}) %collective-permute-start.1) | collective-permute-done | bytes 32800 | tf_op jit(solution)/shard_map/ppermute | solution.py:83
  39.5 0.0 copy-start
  39.6 22.7 %all_to_all.22.all_ref = bf16[16,64,128]{2,1,0:T(8,128)(2,1)S(1)} all-to-all(bf16[16,64,128]{2,1,0:T(8,128)(2,1)S(1)} %shard_map.50), channel_id=1, replica_groups=mesh['tm'=16,'chan'=16] {'tm'}, dimensions={0} | all-to-all | bytes 524288 | tf_op jit(solution)/shard_map/all_to_all | solution.py:105
  62.3 0.0 copy-done
  62.3 4.7 %shard_map.51 = bf16[16,256,128]{2,1,0:T(8,128)(2,1)S(1)} custom-call(bf16[16,64,128]{2,1,0:T(8,128)(2,1)S(1)} %all_to_all.22.all_ref, bf16[1728,256]{1,0:T(8,128)(2,1)S(1)} %bitcast.10), custom_call_target="tpu_custom_call" | custom-call | tf_op jit(solution)/shard_map/pallas_call | solution.py:207
  67.0 20.3 %all_to_all.23.parts_ref = bf16[16,256,128]{2,1,0:T(8,128)(2,1)S(1)} all-to-all(bf16[16,256,128]{2,1,0:T(8,128)(2,1)S(1)} %shard_map.51), channel_id=1, replica_groups=mesh['tm'=16,'chan'=16] {'chan'}, dimensions={0} | all-to-all | bytes 2097152 | tf_op jit(solution)/shard_map/all_to_all | solution.py:213
  87.4 1.2 %shard_map.52 = bf16[2,32,512]{2,1,0:T(8,128)(2,1)} custom-call(bf16[16,256,128]{2,1,0:T(8,128)(2,1)S(1)} %all_to_all.23.parts_ref), custom_call_target="tpu_custom_call" | custom-call | tf_op jit(solution)/shard_map/pallas_call | solution.py:214
  (2 shorter events, 0.0 us)
Async XLA Ops:
  0.0 0.8 copy-start.3
  0.8 15.2 %copy-start.1 = (bf16[64,27,1024]{2,0,1:T(8,128)(2,1)S(1)}, bf16[64,27,1024]{2,0,1:T(8,128)(2,1)}, u32[]{:S(2)}) copy-start(bf16[64,27,1024]{2,0,1:T(8,128)(2,1)} %param.5) | copy-start | bytes 10616836
  17.4 4.6 %collective-permute-start = (f32[64,128]{1,0:T(8,128)S(1)}, f32[64,128]{1,0:T(8,128)S(1)}, u32[]{:S(2)}, u32[]{:S(2)}) collective-permute-start(f32[64,128]{1,0:T(8,128)S(1)} %get-tuple-element.13), channel_id=1, source_target_pairs={{0,16},{16,32},{32,48},{48,64},{64,80},{80,96},{96,112},{112,128},... | collective-permute-start | bytes 98312 | tf_op jit(solution)/shard_map/ppermute | solution.py:83
  22.0 10.8 %copy-start.2 = (bf16[64,27,1024]{2,0,1:T(8,128)(2,1)S(1)}, bf16[64,27,1024]{2,0,1:T(8,128)(2,1)}, u32[]{:S(2)}) copy-start(bf16[64,27,1024]{2,0,1:T(8,128)(2,1)} %param.6) | copy-start | bytes 10616836
  34.2 5.4 %collective-permute-start.1 = (f32[64,128]{1,0:T(8,128)S(1)}, f32[64,128]{1,0:T(8,128)S(1)}, u32[]{:S(2)}, u32[]{:S(2)}) collective-permute-start(f32[64,128]{1,0:T(8,128)S(1)} %get-tuple-element.15), channel_id=1, source_target_pairs={{0,16},{16,32},{32,48},{48,64},{64,80},{80,96},{96,112},{112,128},... | collective-permute-start | bytes 98312 | tf_op jit(solution)/shard_map/ppermute | solution.py:83
  39.5 22.8 %copy-start = (bf16[27,64,256]{2,1,0:T(8,128)(2,1)S(1)}, bf16[27,64,256]{2,1,0:T(8,128)(2,1)}, u32[]{:S(2)}) copy-start(bf16[27,64,256]{2,1,0:T(8,128)(2,1)} %param.7) | copy-start | bytes 2654212

commit v3 on v2

v3 whole, which is shorter than its diff:
```python
import jax
import jax.numpy as jnp
import numpy as np
from jax import lax
from jax.experimental import pallas as pl
from jax.experimental.pallas import tpu as pltpu
from jax.sharding import PartitionSpec as P

EPSILON = 1e-06
F32 = jnp.float32
BF16 = jnp.bfloat16
COLS = 4
FRAMES = 2
CELL = FRAMES * COLS
LANES = 128
ROWS = 16
PAIR = 4
BAND = 4
BANDS = 2
MIB = 1 << 20


def lane_ids():
    lane = lax.broadcasted_iota(jnp.int32, (1, LANES), 1)
    return lane // CELL, (lane // COLS) % FRAMES, lane % COLS


def spatial_sum(product, first_tap, outs):
    row, _, col = lane_ids()
    total = None
    for row_off in range(3):
        part = None
        for col_off in range(3):
            start = (first_tap + 3 * row_off + col_off) * outs
            piece = product[start : start + outs]
            if col_off == 0:
                piece = jnp.where(col >= 1, pltpu.roll(piece, 1, 1), 0.0)
            if col_off == 2:
                piece = jnp.where(col < COLS - 1, pltpu.roll(piece, LANES - 1, 1), 0.0)
            part = piece if part is None else part + piece
        if row_off == 0:
            part = jnp.where(row >= 1, pltpu.roll(part, CELL, 1), 0.0)
        if row_off == 2:
            part = jnp.where(row < ROWS - 1, pltpu.roll(part, LANES - CELL, 1), 0.0)
        total = part if total is None else total + part
    return total


def start_kernel(latent_ref, places_ref, copies_ref):
    cells = [latent_ref[t, r] for r in range(ROWS) for t in range(FRAMES)]
    places = jnp.concatenate(cells, axis=0).astype(F32).T.astype(BF16)
    places_ref[...] = places
    for i in range(copies_ref.shape[0]):
        copies_ref[i] = places


def block_kernel(whole_ref, weight_ref, *rest):
    *residual, own_ref, later_ref = rest
    depth = whole_ref.shape[0]
    outs = own_ref.shape[0]
    values = whole_ref[...].astype(F32)
    squares = jnp.sum(values * values, axis=0, keepdims=True)
    scaled = values * lax.rsqrt(squares / depth + EPSILON)
    act = (scaled / (1.0 + jnp.exp(-scaled))).astype(BF16)
    product = jnp.dot(weight_ref[...], act, preferred_element_type=F32)
    frame = lane_ids()[1]
    oldest = spatial_sum(product, 0, outs)
    middle = spatial_sum(product, 9, outs)
    newest = spatial_sum(product, 18, outs)
    first = lax.axis_index("tm") == 0
    start = jnp.where(frame == 0, middle + oldest, pltpu.roll(oldest, COLS, 1))
    own = newest + jnp.where(frame == 1, pltpu.roll(middle, COLS, 1), 0.0)
    own = own + jnp.where(first, start, 0.0)
    for ref in residual:
        own = ref[...].astype(F32) + own
    own_ref[...] = own
    later_ref[...] = oldest + jnp.where(frame == 0, pltpu.roll(middle, LANES - COLS, 1), 0.0)


def block_conv(whole, weight, outs, *residual):
    shape = jax.ShapeDtypeStruct((outs, LANES), F32)
    return pl.pallas_call(
        block_kernel,
        out_shape=(shape, shape),
        compiler_params=pltpu.CompilerParams(vmem_limit_bytes=16 * MIB),
        cost_estimate=pl.CostEstimate(flops=4 * 10**9, bytes_accessed=8 * MIB, transcendentals=0),
    )(whole, weight, *residual)


def next_frames(i):
    return (i + 1) % lax.axis_size("tm")


def shifted_on(later):
    return lax.ppermute(later, "tm", [(i, next_frames(i)) for i in range(lax.axis_size("tm"))])


def swapped(value):
    return lax.ppermute(value, "chan", [(c, c ^ PAIR) for c in range(lax.axis_size("chan"))])


def shifted_and_swapped(later):
    frames, channels = lax.axis_size("tm"), lax.axis_size("chan")
    pairs = [
        (i * channels + c, next_frames(i) * channels + (c ^ PAIR))
        for i in range(frames)
        for c in range(channels)
    ]
    return lax.ppermute(later, ("tm", "chan"), pairs)


def summed(own_ref, earlier_ref):
    earlier = jnp.where(lax.axis_index("tm") == 0, 0.0, earlier_ref[...])
    return (own_ref[...] + earlier).astype(BF16)


def hidden_kernel(own_ref, earlier_ref, copies_ref):
    value = summed(own_ref, earlier_ref)
    for i in range(copies_ref.shape[0]):
        copies_ref[i] = value


def bands_kernel(own_ref, earlier_ref, own_too_ref, earlier_too_ref, copies_ref, padded):
    both = [summed(own_ref, earlier_ref), summed(own_too_ref, earlier_too_ref)]
    edge = jnp.zeros((CELL, padded.shape[1]), F32)
    padded[0:CELL] = edge
    padded[CELL + LANES :] = edge
    padded[CELL : CELL + LANES] = jnp.concatenate([v.astype(F32).T for v in both], axis=1)
    half = (lax.axis_index("chan") // PAIR) % 2
    bands = []
    for band in range(BANDS):
        first = pl.multiple_of((BAND * half + 2 * BAND * band) * CELL, CELL)
        bands.append(padded[pl.ds(first, (BAND + 2) * CELL), :])
    value = jnp.concatenate(bands, axis=0).astype(BF16)
    for i in range(copies_ref.shape[0]):
        copies_ref[i] = value


def hint(limit):
    return {
        "compiler_params": pltpu.CompilerParams(vmem_limit_bytes=limit * MIB),
        "cost_estimate": pl.CostEstimate(flops=8 * 10**9, bytes_accessed=MIB, transcendentals=0),
    }


def upsample_kernel(all_ref, move_ref, weight_ref, weight_too_ref, out_ref, moved):
    count = 2 * all_ref.shape[1]
    channels = all_ref.shape[3]
    rows = BAND + 2
    for band in range(BANDS):
        for row in range(0, rows, 2):
            places = []
            for r in (row, row + 1):
                start = (band * rows + r) * CELL
                places.append(
                    jnp.concatenate(
                        [all_ref[i % 2, i // 2, start : start + CELL].astype(F32) for i in range(count)],
                        axis=0,
                    )
                )
            pair = jnp.concatenate(places, axis=1).astype(BF16)
            result = jnp.dot(move_ref[...], pair, preferred_element_type=F32).astype(BF16)
            for k in range(9):
                for j in range(2):
                    moved[k, band, (row + j) * LANES : (row + j + 1) * LANES] = result[
                        k * LANES : (k + 1) * LANES, j * channels : (j + 1) * channels
                    ]
    blocks = []
    for tap in range(27):
        blocks.append(weight_ref[tap])
        blocks.append(weight_too_ref[tap])
    weight = jnp.concatenate(blocks, axis=0)
    for band in range(BANDS):
        spread = jnp.concatenate(
            [
                moved[3 * kt + ks, band, kr * LANES : (kr + BAND) * LANES]
                for kt in range(3)
                for kr in range(3)
                for ks in range(3)
            ],
            axis=1,
        )
        result = jnp.dot(spread, weight, preferred_element_type=F32).astype(BF16)
        for r in range(BAND):
            out_ref[band * BAND + r] = result[r * LANES : (r + 1) * LANES]


def moves():
    place = np.arange(LANES)
    frame, col = place // COLS, place % COLS
    blocks = []
    for frame_off in range(3):
        for col_off in range(3):
            target = col + col_off - 1
            source = np.maximum(frame + frame_off - 2, 0) * COLS + target
            fits = (target >= 0) & (target < COLS)
            blocks.append(fits[:, None] & (source[:, None] == place[None, :]))
    return np.concatenate(blocks, axis=0).astype(jnp.bfloat16)


def finish_kernel(parts_ref, out_ref, total_ref):
    count = parts_ref.shape[0]
    channels = out_ref.shape[1]
    total = parts_ref[0].astype(F32)
    for i in range(1, count):
        total = total + parts_ref[i].astype(F32)
    total_ref[...] = total.T
    wide = out_ref.shape[2]
    source = lax.broadcasted_iota(jnp.int32, (LANES, wide), 0)
    target = lax.broadcasted_iota(jnp.int32, (LANES, wide), 1)
    base = (source // COLS) * (4 * COLS) + (source % COLS) * 2
    for p2 in range(2):
        result = jnp.zeros((channels, wide), F32)
        for p1 in range(2):
            for p3 in range(2):
                rows = total_ref[pl.ds(4 * p1 + 2 * p2 + p3, channels, stride=8), :]
                place = jnp.where(target == base + 2 * COLS * p1 + p3, 1.0, 0.0).astype(BF16)
                result = result + jnp.dot(rows.astype(BF16), place, preferred_element_type=F32)
        out_ref[p2] = result.astype(BF16)


def on_device(latent, conv_first, conv_second, conv_upsample):
    channels = latent.shape[1]
    frames_on, channels_on = lax.axis_size("tm"), lax.axis_size("chan")

    def taps(weight):
        outs, count, depth = weight.shape
        return jnp.transpose(weight, (1, 0, 2)).reshape(count * outs, depth)

    shape = (channels, LANES)
    places, copies = pl.pallas_call(
        start_kernel,
        out_shape=(
            jax.ShapeDtypeStruct(shape, BF16),
            jax.ShapeDtypeStruct((channels_on,) + shape, BF16),
        ),
        **hint(8),
    )(jnp.transpose(latent, (0, 2, 3, 1)))
    whole = lax.all_to_all(copies, "chan", 0, 0, tiled=True).reshape(-1, LANES)

    own, later = block_conv(whole, taps(conv_first), channels)
    copies = pl.pallas_call(
        hidden_kernel, out_shape=jax.ShapeDtypeStruct((channels_on,) + shape, BF16), **hint(8)
    )(own, shifted_on(later))
    whole = lax.all_to_all(copies, "chan", 0, 0, tiled=True).reshape(-1, LANES)

    own, later = block_conv(whole, taps(conv_second), channels, places)
    own_too = swapped(own)
    earlier_too = shifted_and_swapped(later)
    earlier = shifted_on(later)
    earlier, other = lax.optimization_barrier((earlier, conv_upsample))
    other = swapped(other)
    packed = (BANDS * (BAND + 2) * CELL, 2 * channels)
    copies = pl.pallas_call(
        bands_kernel,
        out_shape=jax.ShapeDtypeStruct((frames_on // 2,) + packed, BF16),
        scratch_shapes=[pltpu.VMEM((LANES + 2 * CELL, 2 * channels), F32)],
        **hint(8),
    )(own, earlier, own_too, earlier_too)
    along = [list(range(core, frames_on, 2)) for core in range(2)]
    cores = [[i, i + 1] for i in range(0, frames_on, 2)]
    frames = lax.all_to_all(copies, "tm", 0, 0, tiled=True, axis_index_groups=along)
    frames = lax.all_gather(frames, "tm", axis_index_groups=cores)

    outs = conv_upsample.shape[2]
    rows_here = BANDS * BAND
    partial = pl.pallas_call(
        upsample_kernel,
        out_shape=jax.ShapeDtypeStruct((rows_here, LANES, outs), BF16),
        scratch_shapes=[pltpu.VMEM((9, BANDS, (BAND + 2) * LANES, 2 * channels), BF16)],
        compiler_params=pltpu.CompilerParams(vmem_limit_bytes=32 * MIB),
    )(frames, moves(), conv_upsample, other)
    groups = [[c for c in range(channels_on) if (c // PAIR) % 2 == half] for half in range(2)]
    parts = lax.all_to_all(partial, "chan", 0, 0, tiled=True, axis_index_groups=groups)
    return pl.pallas_call(
        finish_kernel,
        out_shape=jax.ShapeDtypeStruct((2, outs // 8, 4 * LANES), BF16),
        scratch_shapes=[pltpu.VMEM((outs, LANES), F32)],
        compiler_params=pltpu.CompilerParams(vmem_limit_bytes=16 * MIB),
    )(parts)


def solution(mesh):
    placed = (
        P("tm", "chan", None, None),
        P("chan", None, None),
        P("chan", None, None),
        P(None, "chan", "tm"),
    )
    return jax.shard_map(
        on_device, mesh=mesh, in_specs=placed, out_specs=P("chan", "tm", None), check_vma=False
    )
```

time: 88.8 us -> 81.8 us (0.921)
  blocking collectives: 68.9 us -> 59.7 us
  waiting for transfers between devices: 2.58 us -> 4.81 us
  Pallas kernels: 8.87 us -> 7.21 us
  starting transfers between devices: 7.35 us -> 8.93 us
    all_to_all x3 -> x2, blocking collectives: 53.8 us -> 29 us  [the longest x1 15.1 us: on_device(): lax.all_to_all(copies, 'tm', 0, 0, tiled=True, axis_index_groups=along)]
    all_to_all x1 -> x2, blocking collectives: 15.1 us -> 25.8 us  [on_device(): whole = lax.all_to_all(copies, 'chan', 0, 0, tiled=True).reshape(-1, LANES)]
    all_gather x0 -> x1, blocking collectives: none -> 4.86 us  [on_device(): frames = lax.all_gather(frames, 'tm', axis_index_groups=cores)]
    ppermute x2 -> x5, waiting for transfers between devices: 2.58 us -> 4.81 us  [the longest x1 2.6 us: shifted_and_swapped(): return lax.ppermute(later, ('tm', 'chan'), pairs)]
    pallas_call x3, Pallas kernels: 4.77 us -> 3.16 us  [the longest x1 2.95 us: on_device(): pl.pallas_call(upsample_kernel, out_shape=jax.ShapeDtypeStruct((rows_here...]
    ppermute x2 -> x5, starting transfers between devices: 7.35 us -> 8.93 us  [the longest x2 7.35 us: shifted_on(): lax.ppermute(later, 'tm', [(i, next_frames(i)) for i in range(lax.axis_si...]
  transfers between devices with their start and end apart: 2 -> 5, of which waited for: 2 -> 3; matrix products, arithmetic and copies ran while one was open for 0% -> 0% of each run, Pallas kernels for 0% -> 0%
where the time goes in v3:
time: 81.8 us; the launch traced here: 81.5 us
  blocking collectives  59.7 us (73%)
  starting transfers between devices  8.93 us (11%)
  Pallas kernels  7.21 us (9%)
  waiting for transfers between devices  4.81 us (6%)
    all_to_all x2, blocking collectives, on_device(): whole = lax.all_to_all(copies, 'chan', 0, 0, tiled=True).reshape(-1, LANES)  25.8 us
    all_to_all x1, blocking collectives, on_device(): lax.all_to_all(copies, 'tm', 0, 0, tiled=True, axis_index_groups=along)  15.1 us
    all_to_all x1, blocking collectives, on_device(): lax.all_to_all(partial, 'chan', 0, 0, tiled=True, axis_index_groups=groups)  14 us
    ppermute x2, starting transfers between devices, shifted_on(): lax.ppermute(later, 'tm', [(i, next_frames(i)) for i in range(lax.axis_si...  7.35 us
    all_gather x1, blocking collectives, on_device(): frames = lax.all_gather(frames, 'tm', axis_index_groups=cores)  4.86 us
    pallas_call x1, Pallas kernels, on_device(): pl.pallas_call(upsample_kernel, out_shape=jax.ShapeDtypeStruct((rows_here...  2.95 us
    pallas_call x2, Pallas kernels, block_conv(): pl.pallas_call(block_kernel, out_shape=(shape, shape), compiler_params=pl...  2.86 us
    ppermute x1, waiting for transfers between devices, shifted_and_swapped(): return lax.ppermute(later, ('tm', 'chan'), pairs)  2.6 us
  transfers between devices with their start and end apart: 5, of which 3 were waited for; matrix products, arithmetic and copies ran while one was open for 0% of the time, Pallas kernels for 0%

profile of v3, /device:TPU:1, one launch (start us, length us, event | category | flops | bytes accessed | tf_op | source)
XLA Modules:
  0.0 81.5 jit_solution(17465887470175719219)
XLA Ops:
  0.0 0.8 copy-done.4
  0.8 0.1 shard_map.55
  0.9 15.1 %all_to_all.20 = bf16[16,64,128]{2,1,0:T(8,128)(2,1)S(1)} all-to-all(bf16[16,64,128]{2,1,0:T(8,128)(2,1)S(1)} %get-tuple-element.13), channel_id=1, replica_groups=mesh['tm'=16,'chan'=16] {'chan'}, dimensions={0} | all-to-all | bytes 524288 | tf_op jit(solution)/shard_map/all_to_all | solution.py:239
  16.0 0.0 copy-done.2
  16.0 1.4 %shard_map.56 = (f32[64,128]{1,0:T(8,128)S(1)}, f32[64,128]{1,0:T(8,128)S(1)}) custom-call(bf16[1024,128]{1,0:T(8,128)(2,1)S(1)} %bitcast.12, bf16[1728,1024]{1,0:T(8,128)(2,1)S(1)} %bitcast.13), custom_call_target="tpu_custom_call" | custom-call | flops 4000000000 | bytes 8388608 | tf_op jit(solution)/shard_map/pallas_call | solution.py:82
  17.4 3.5 %collective-permute-start = (f32[64,128]{1,0:T(8,128)S(1)}, f32[64,128]{1,0:T(8,128)S(1)}, u32[]{:S(2)}, u32[]{:S(2)}) collective-permute-start(f32[64,128]{1,0:T(8,128)S(1)} %get-tuple-element.15), channel_id=1, source_target_pairs={{0,16},{16,32},{32,48},{48,64},{64,80},{80,96},{96,112},{112,128},... | collective-permute-start | bytes 98312 | tf_op jit(solution)/shard_map/ppermute | solution.py:95
  21.0 1.0 %collective-permute-done.earlier_ref = f32[64,128]{1,0:T(8,128)S(1)} collective-permute-done((f32[64,128]{1,0:T(8,128)S(1)}, f32[64,128]{1,0:T(8,128)S(1)}, u32[]{:S(2)}, u32[]{:S(2)}) %collective-permute-start) | collective-permute-done | bytes 32800 | tf_op jit(solution)/shard_map/ppermute | solution.py:95
  22.0 10.7 %all_to_all.21 = bf16[16,64,128]{2,1,0:T(8,128)(2,1)S(1)} all-to-all(bf16[16,64,128]{2,1,0:T(8,128)(2,1)S(1)} %shard_map.57), channel_id=1, replica_groups=mesh['tm'=16,'chan'=16] {'chan'}, dimensions={0} | all-to-all | bytes 524288 | tf_op jit(solution)/shard_map/all_to_all | solution.py:245
  32.7 0.0 copy-done.3
  32.7 1.4 %shard_map.58 = (f32[64,128]{1,0:T(8,128)S(1)}, f32[64,128]{1,0:T(8,128)S(1)}) custom-call(bf16[1024,128]{1,0:T(8,128)(2,1)S(1)} %bitcast.11, bf16[1728,1024]{1,0:T(8,128)(2,1)S(1)} %bitcast.14, bf16[64,128]{1,0:T(8,128)(2,1)S(1)} %get-tuple-element.16.rest_0_), custom_call_target="tpu_custom_call" | custom-call | flops 4000000000 | bytes 8388608 | tf_op jit(solution)/shard_map/pallas_call | solution.py:82
  34.2 3.8 %collective-permute-start.1 = (f32[64,128]{1,0:T(8,128)S(1)}, f32[64,128]{1,0:T(8,128)S(1)}, u32[]{:S(2)}, u32[]{:S(2)}) collective-permute-start(f32[64,128]{1,0:T(8,128)S(1)} %get-tuple-element.18), channel_id=1, source_target_pairs={{0,16},{16,32},{32,48},{48,64},{64,80},{80,96},{96,112},{112,128},... | collective-permute-start | bytes 98312 | tf_op jit(solution)/shard_map/ppermute | solution.py:95
  38.0 0.0 collective-permute-start.2
  38.0 1.6 %collective-permute-start.3 = (f32[64,128]{1,0:T(8,128)S(1)}, f32[64,128]{1,0:T(8,128)S(1)}, u32[]{:S(2)}, u32[]{:S(2)}) collective-permute-start(f32[64,128]{1,0:T(8,128)S(1)} %get-tuple-element.18), channel_id=1, source_target_pairs={{0,20},{1,21},{2,22},{3,23},{4,16},{5,17},{6,18},{7,19},{8,28},{9,... | collective-permute-start | bytes 98312 | tf_op jit(solution)/shard_map/ppermute | solution.py:109
  39.6 0.0 collective-permute-done.1.earlier_ref
  39.6 0.0 collective-permute-start.4
  39.6 1.2 %collective-permute-done.2.own_too_ref = f32[64,128]{1,0:T(8,128)S(1)} collective-permute-done((f32[64,128]{1,0:T(8,128)S(1)}, f32[64,128]{1,0:T(8,128)S(1)}, u32[]{:S(2)}, u32[]{:S(2)}) %collective-permute-start.2) | collective-permute-done | bytes 32800 | tf_op jit(solution)/shard_map/ppermute | solution.py:99
  40.8 2.6 %collective-permute-done.3.earlier_too_ref = f32[64,128]{1,0:T(8,128)S(1)} collective-permute-done((f32[64,128]{1,0:T(8,128)S(1)}, f32[64,128]{1,0:T(8,128)S(1)}, u32[]{:S(2)}, u32[]{:S(2)}) %collective-permute-start.3) | collective-permute-done | bytes 32800 | tf_op jit(solution)/shard_map/ppermute | solution.py:109
  43.4 0.2 shard_map.59
  43.5 15.1 %all_to_all.22 = bf16[8,96,128]{2,1,0:T(8,128)(2,1)S(1)} all-to-all(bf16[8,96,128]{2,1,0:T(8,128)(2,1)S(1)} %shard_map.59), channel_id=1, replica_groups={{0,32,64,96,128,160,192,224},{16,48,80,112,144,176,208,240},{1,33,65,97..., dimensions={0} | all-to-all | bytes 393216 | tf_op jit(solution)/shard_map/all_to_all | solution.py:262
  58.6 4.9 %all-gather = bf16[16,96,128]{2,1,0:T(8,128)(2,1)S(1)} all-gather(bf16[8,96,128]{2,1,0:T(8,128)(2,1)S(1)} %all_to_all.22), channel_id=2, replica_groups={{0,16},{32,48},{64,80},{96,112},{128,144},{160,176},{192,208},{224,240}..., dimensions={0}, use_global_device_ids=true | all-gather | bytes 589824 | tf_op jit(solution)/shard_map/all_gather | solution.py:263
  63.5 0.0 collective-permute-done.4.weight_too_ref
  63.5 3.0 %shard_map.60 = bf16[8,128,256]{2,1,0:T(8,128)(2,1)S(1)} custom-call(bf16[2,8,96,128]{3,2,1,0:T(8,128)(2,1)S(1)} %bitcast.10, bf16[1152,128]{1,0:T(8,128)(2,1)S(1)} %copy-done.1, bf16[27,64,256]{2,1,0:T(8,128)(2,1)S(1)} %copy-done, bf16[27,64,256]{2,1,0:T(8,128)(2,1)S(1)} %collective-permute-done.4.weight_too_ref), custom_call_target="tpu_custom_call" | custom-call | tf_op jit(solution)/shard_map/pallas_call | solution.py:267
  66.5 14.0 %all_to_all.23.parts_ref = bf16[8,128,256]{2,1,0:T(8,128)(2,1)S(1)} all-to-all(bf16[8,128,256]{2,1,0:T(8,128)(2,1)S(1)} %shard_map.60), channel_id=1, replica_groups={{0,1,2,3,8,9,10,11},{4,5,6,7,12,13,14,15},{16,17,18,19,24,25,26,27},{20..., dimensions={0} | all-to-all | bytes 1048576 | tf_op jit(solution)/shard_map/all_to_all | solution.py:274
  80.4 1.1 %shard_map.61 = bf16[2,32,512]{2,1,0:T(8,128)(2,1)} custom-call(bf16[8,128,256]{2,1,0:T(8,128)(2,1)S(1)} %all_to_all.23.parts_ref), custom_call_target="tpu_custom_call" | custom-call | tf_op jit(solution)/shard_map/pallas_call | solution.py:275
  (8 shorter events, 0.0 us)
Async XLA Ops:
  0.0 0.8 copy-start.4
  0.8 15.2 %copy-start.2 = (bf16[64,27,1024]{2,0,1:T(8,128)(2,1)S(1)}, bf16[64,27,1024]{2,0,1:T(8,128)(2,1)}, u32[]{:S(2)}) copy-start(bf16[64,27,1024]{2,0,1:T(8,128)(2,1)} %param.6) | copy-start | bytes 10616836
  17.4 4.6 %collective-permute-start = (f32[64,128]{1,0:T(8,128)S(1)}, f32[64,128]{1,0:T(8,128)S(1)}, u32[]{:S(2)}, u32[]{:S(2)}) collective-permute-start(f32[64,128]{1,0:T(8,128)S(1)} %get-tuple-element.15), channel_id=1, source_target_pairs={{0,16},{16,32},{32,48},{48,64},{64,80},{80,96},{96,112},{112,128},... | collective-permute-start | bytes 98312 | tf_op jit(solution)/shard_map/ppermute | solution.py:95
  22.0 10.8 %copy-start.3 = (bf16[64,27,1024]{2,0,1:T(8,128)(2,1)S(1)}, bf16[64,27,1024]{2,0,1:T(8,128)(2,1)}, u32[]{:S(2)}) copy-start(bf16[64,27,1024]{2,0,1:T(8,128)(2,1)} %param.7) | copy-start | bytes 10616836
  32.7 6.8 %copy-start = (bf16[27,64,256]{2,1,0:T(8,128)(2,1)S(1)}, bf16[27,64,256]{2,1,0:T(8,128)(2,1)}, u32[]{:S(2)}) copy-start(bf16[27,64,256]{2,1,0:T(8,128)(2,1)} %weight_ref.1) | copy-start | bytes 2654212
  34.2 5.4 %collective-permute-start.1 = (f32[64,128]{1,0:T(8,128)S(1)}, f32[64,128]{1,0:T(8,128)S(1)}, u32[]{:S(2)}, u32[]{:S(2)}) collective-permute-start(f32[64,128]{1,0:T(8,128)S(1)} %get-tuple-element.18), channel_id=1, source_target_pairs={{0,16},{16,32},{32,48},{48,64},{64,80},{80,96},{96,112},{112,128},... | collective-permute-start | bytes 98312 | tf_op jit(solution)/shard_map/ppermute | solution.py:95
  38.0 25.5 %copy-start.1 = (bf16[1152,128]{1,0:T(8,128)(2,1)S(1)}, bf16[1152,128]{1,0:T(8,128)(2,1)}, u32[]{:S(2)}) copy-start(bf16[1152,128]{1,0:T(8,128)(2,1)} %constant.2.clone.move_ref) | copy-start | bytes 884740
  38.0 2.8 %collective-permute-start.2 = (f32[64,128]{1,0:T(8,128)S(1)}, f32[64,128]{1,0:T(8,128)S(1)}, u32[]{:S(2)}, u32[]{:S(2)}) collective-permute-start(f32[64,128]{1,0:T(8,128)S(1)} %get-tuple-element.17.own_ref), channel_id=1, source_target_pairs={{0,4},{1,5},{2,6},{3,7},{4,0},{5,1},{6,2},{7,3},{8,12},{9,13},{10,... | collective-permute-start | bytes 98312 | tf_op jit(solution)/shard_map/ppermute | solution.py:99
  38.0 5.4 %collective-permute-start.3 = (f32[64,128]{1,0:T(8,128)S(1)}, f32[64,128]{1,0:T(8,128)S(1)}, u32[]{:S(2)}, u32[]{:S(2)}) collective-permute-start(f32[64,128]{1,0:T(8,128)S(1)} %get-tuple-element.18), channel_id=1, source_target_pairs={{0,20},{1,21},{2,22},{3,23},{4,16},{5,17},{6,18},{7,19},{8,28},{9,... | collective-permute-start | bytes 98312 | tf_op jit(solution)/shard_map/ppermute | solution.py:109
  39.6 23.9 %collective-permute-start.4 = (bf16[27,64,256]{2,1,0:T(8,128)(2,1)S(1)}, bf16[27,64,256]{2,1,0:T(8,128)(2,1)S(1)}, u32[]{:S(2)}, u32[]{:S(2)}) collective-permute-start(bf16[27,64,256]{2,1,0:T(8,128)(2,1)S(1)} %copy-done), channel_id=1, source_target_pairs={{0,4},{1,5},{2,6},{3,7},{4,0},{5,1},{6,2},{7,3},{8,12},{9,13},{10,... | collective-permute-start | bytes 2654216 | tf_op jit(solution)/shard_map/ppermute | solution.py:99

commit v4 on v3

--- a/solution.py
+++ b/solution.py
@@ -120,18 +120,19 @@
         copies_ref[i] = value
 
 
-def bands_kernel(own_ref, earlier_ref, own_too_ref, earlier_too_ref, copies_ref, padded):
+def middle():
+    place = lax.axis_index("chan") // PAIR
+    return (place == 1) | (place == 2)
+
+
+def bands_kernel(own_ref, earlier_ref, own_too_ref, earlier_too_ref, copies_ref):
     both = [summed(own_ref, earlier_ref), summed(own_too_ref, earlier_too_ref)]
-    edge = jnp.zeros((CELL, padded.shape[1]), F32)
-    padded[0:CELL] = edge
-    padded[CELL + LANES :] = edge
-    padded[CELL : CELL + LANES] = jnp.concatenate([v.astype(F32).T for v in both], axis=1)
-    half = (lax.axis_index("chan") // PAIR) % 2
-    bands = []
-    for band in range(BANDS):
-        first = pl.multiple_of((BAND * half + 2 * BAND * band) * CELL, CELL)
-        bands.append(padded[pl.ds(first, (BAND + 2) * CELL), :])
-    value = jnp.concatenate(bands, axis=0).astype(BF16)
+    places = jnp.concatenate([v.astype(F32).T for v in both], axis=1)
+    near, far = (BAND - 1) * CELL, (3 * BAND - 1) * CELL
+    count = copies_ref.shape[1]
+    inner = places[near : near + count]
+    outer = jnp.concatenate([places[far:], places[: count - (LANES - far)]], axis=0)
+    value = jnp.where(middle(), inner, outer).astype(BF16)
     for i in range(copies_ref.shape[0]):
         copies_ref[i] = value
 
@@ -146,25 +147,27 @@
 def upsample_kernel(all_ref, move_ref, weight_ref, weight_too_ref, out_ref, moved):
     count = 2 * all_ref.shape[1]
     channels = all_ref.shape[3]
-    rows = BAND + 2
-    for band in range(BANDS):
-        for row in range(0, rows, 2):
-            places = []
-            for r in (row, row + 1):
-                start = (band * rows + r) * CELL
-                places.append(
-                    jnp.concatenate(
-                        [all_ref[i % 2, i // 2, start : start + CELL].astype(F32) for i in range(count)],
-                        axis=0,
-                    )
-                )
-            pair = jnp.concatenate(places, axis=1).astype(BF16)
-            result = jnp.dot(move_ref[...], pair, preferred_element_type=F32).astype(BF16)
-            for k in range(9):
-                for j in range(2):
-                    moved[k, band, (row + j) * LANES : (row + j + 1) * LANES] = result[
-                        k * LANES : (k + 1) * LANES, j * channels : (j + 1) * channels
-                    ]
+    inner = jnp.where(middle(), 1.0, 0.0).astype(BF16)
+    for row in range(0, BANDS * BAND + 2, 2):
+        places = []
+        for r in (row, row + 1):
+            cells = [
+                all_ref[i % 2, i // 2, r * CELL : (r + 1) * CELL].astype(F32)
+                for i in range(count)
+            ]
+            places.append(jnp.concatenate(cells, axis=0))
+        pair = jnp.concatenate(places, axis=1).astype(BF16)
+        result = jnp.dot(move_ref[...], pair, preferred_element_type=F32).astype(BF16)
+        for k in range(9):
+            for j in range(2):
+                piece = result[k * LANES : (k + 1) * LANES, j * channels : (j + 1) * channels]
+                for band in range(BANDS):
+                    at = row + j - band * BAND
+                    if 0 <= at < BAND + 2:
+                        seam = at == (BAND + 1 if band == 0 else 0)
+                        moved[k, band, at * LANES : (at + 1) * LANES] = (
+                            piece * inner if seam else piece
+                        )
     blocks = []
     for tap in range(27):
         blocks.append(weight_ref[tap])
@@ -198,25 +201,36 @@
     return np.concatenate(blocks, axis=0).astype(jnp.bfloat16)
 
 
-def finish_kernel(parts_ref, out_ref, total_ref):
+def finish_kernel(parts_ref, spread_ref, out_ref, total_ref):
     count = parts_ref.shape[0]
     channels = out_ref.shape[1]
     total = parts_ref[0].astype(F32)
     for i in range(1, count):
         total = total + parts_ref[i].astype(F32)
     total_ref[...] = total.T
-    wide = out_ref.shape[2]
-    source = lax.broadcasted_iota(jnp.int32, (LANES, wide), 0)
-    target = lax.broadcasted_iota(jnp.int32, (LANES, wide), 1)
-    base = (source // COLS) * (4 * COLS) + (source % COLS) * 2
+    halves = []
     for p2 in range(2):
-        result = jnp.zeros((channels, wide), F32)
-        for p1 in range(2):
-            for p3 in range(2):
-                rows = total_ref[pl.ds(4 * p1 + 2 * p2 + p3, channels, stride=8), :]
-                place = jnp.where(target == base + 2 * COLS * p1 + p3, 1.0, 0.0).astype(BF16)
-                result = result + jnp.dot(rows.astype(BF16), place, preferred_element_type=F32)
-        out_ref[p2] = result.astype(BF16)
+        pieces = [
+            total_ref[pl.ds(4 * p1 + 2 * p2 + p3, channels, stride=8), :]
+            for p1 in range(2)
+            for p3 in range(2)
+        ]
+        halves.append(jnp.concatenate(pieces, axis=1))
+    value = jnp.concatenate(halves, axis=0).astype(BF16)
+    result = jnp.dot(value, spread_ref[...], preferred_element_type=F32).astype(BF16)
+    for p2 in range(2):
+        out_ref[p2] = result[p2 * channels : (p2 + 1) * channels]
+
+
+def spreads():
+    place = np.arange(LANES)
+    target = np.arange(4 * LANES)
+    base = (place // COLS) * (4 * COLS) + (place % COLS) * 2
+    blocks = []
+    for p1 in range(2):
+        for p3 in range(2):
+            blocks.append((base + 2 * COLS * p1 + p3)[:, None] == target[None, :])
+    return np.concatenate(blocks, axis=0).astype(jnp.bfloat16)
 
 
 def on_device(latent, conv_first, conv_second, conv_upsample):
@@ -248,13 +262,12 @@
     own_too = swapped(own)
     earlier_too = shifted_and_swapped(later)
     earlier = shifted_on(later)
-    earlier, other = lax.optimization_barrier((earlier, conv_upsample))
+    earlier_too, other = lax.optimization_barrier((earlier_too, conv_upsample))
     other = swapped(other)
-    packed = (BANDS * (BAND + 2) * CELL, 2 * channels)
+    packed = ((BANDS * BAND + 2) * CELL, 2 * channels)
     copies = pl.pallas_call(
         bands_kernel,
         out_shape=jax.ShapeDtypeStruct((frames_on // 2,) + packed, BF16),
-        scratch_shapes=[pltpu.VMEM((LANES + 2 * CELL, 2 * channels), F32)],
         **hint(8),
     )(own, earlier, own_too, earlier_too)
     along = [list(range(core, frames_on, 2)) for core in range(2)]
@@ -270,14 +283,16 @@
         scratch_shapes=[pltpu.VMEM((9, BANDS, (BAND + 2) * LANES, 2 * channels), BF16)],
         compiler_params=pltpu.CompilerParams(vmem_limit_bytes=32 * MIB),
     )(frames, moves(), conv_upsample, other)
-    groups = [[c for c in range(channels_on) if (c // PAIR) % 2 == half] for half in range(2)]
+    groups = [
+        [place * PAIR + c for place in pair for c in range(PAIR)] for pair in ((1, 2), (3, 0))
+    ]
     parts = lax.all_to_all(partial, "chan", 0, 0, tiled=True, axis_index_groups=groups)
     return pl.pallas_call(
         finish_kernel,
         out_shape=jax.ShapeDtypeStruct((2, outs // 8, 4 * LANES), BF16),
         scratch_shapes=[pltpu.VMEM((outs, LANES), F32)],
         compiler_params=pltpu.CompilerParams(vmem_limit_bytes=16 * MIB),
-    )(parts)
+    )(parts, spreads())
 
 
 def solution(mesh):

time: 81.8 us -> 80.2 us (0.980)
  waiting for transfers between devices: 4.81 us -> 2.33 us
  starting transfers between devices: 8.93 us -> 10.1 us
    ppermute x2, starting transfers between devices: 7.35 us -> 3.55 us  [shifted_on(): lax.ppermute(later, 'tm', [(i, next_frames(i)) for i in range(lax.axis_si...]
    ppermute x2, starting transfers between devices: 0.01 us -> 3.04 us  [swapped(): lax.ppermute(value, 'chan', [(c, c ^ PAIR) for c in range(lax.axis_size('...]
    ppermute x1, starting transfers between devices: 1.57 us -> 3.52 us  [shifted_and_swapped(): return lax.ppermute(later, ('tm', 'chan'), pairs)]
    ppermute x1, waiting for transfers between devices: 2.6 us -> 1.3 us  [shifted_and_swapped(): return lax.ppermute(later, ('tm', 'chan'), pairs)]
    ppermute x2, waiting for transfers between devices: 1.18 us -> 0.01 us  [swapped(): lax.ppermute(value, 'chan', [(c, c ^ PAIR) for c in range(lax.axis_size('...]
    all_to_all x1, blocking collectives: 14 us -> 12.8 us  [on_device(): lax.all_to_all(partial, 'chan', 0, 0, tiled=True, axis_index_groups=groups)]
    all_gather x1, blocking collectives: 4.86 us -> 5.87 us  [on_device(): frames = lax.all_gather(frames, 'tm', axis_index_groups=cores)]
  transfers between devices with their start and end apart: 5 -> 5, of which waited for: 3 -> 2; matrix products, arithmetic and copies ran while one was open for 0% -> 0% of each run, Pallas kernels for 0% -> 0%
where the time goes in v4:
time: 80.2 us; the launch traced here: 79.7 us
  blocking collectives  59.5 us (74%)
  starting transfers between devices  10.1 us (13%)
  Pallas kernels  6.91 us (9%)
  waiting for transfers between devices  2.33 us (3%)
    all_to_all x2, blocking collectives, on_device(): whole = lax.all_to_all(copies, 'chan', 0, 0, tiled=True).reshape(-1, LANES)  25.8 us
    all_to_all x1, blocking collectives, on_device(): lax.all_to_all(copies, 'tm', 0, 0, tiled=True, axis_index_groups=along)  15 us
    all_to_all x1, blocking collectives, on_device(): lax.all_to_all(partial, 'chan', 0, 0, tiled=True, axis_index_groups=groups)  12.8 us
    all_gather x1, blocking collectives, on_device(): frames = lax.all_gather(frames, 'tm', axis_index_groups=cores)  5.87 us
    ppermute x2, starting transfers between devices, shifted_on(): lax.ppermute(later, 'tm', [(i, next_frames(i)) for i in range(lax.axis_si...  3.55 us
    ppermute x1, starting transfers between devices, shifted_and_swapped(): return lax.ppermute(later, ('tm', 'chan'), pairs)  3.52 us
    ppermute x2, starting transfers between devices, swapped(): lax.ppermute(value, 'chan', [(c, c ^ PAIR) for c in range(lax.axis_size('...  3.04 us
    pallas_call x2, Pallas kernels, block_conv(): pl.pallas_call(block_kernel, out_shape=(shape, shape), compiler_params=pl...  2.86 us
  transfers between devices with their start and end apart: 5, of which 2 were waited for; matrix products, arithmetic and copies ran while one was open for 0% of the time, Pallas kernels for 0%

profile of v4, /device:TPU:1, one launch (start us, length us, event | category | flops | bytes accessed | tf_op | source)
XLA Modules:
  0.0 79.7 jit_solution(7285483209582206124)
XLA Ops:
  0.0 0.8 copy-done.5
  0.8 0.1 shard_map.64
  0.9 15.1 %all_to_all.20 = bf16[16,64,128]{2,1,0:T(8,128)(2,1)S(1)} all-to-all(bf16[16,64,128]{2,1,0:T(8,128)(2,1)S(1)} %get-tuple-element.13), channel_id=1, replica_groups=mesh['tm'=16,'chan'=16] {'chan'}, dimensions={0} | all-to-all | bytes 524288 | tf_op jit(solution)/shard_map/all_to_all | solution.py:253
  16.0 0.0 copy-done.3
  16.0 1.4 %shard_map.65 = (f32[64,128]{1,0:T(8,128)S(1)}, f32[64,128]{1,0:T(8,128)S(1)}) custom-call(bf16[1024,128]{1,0:T(8,128)(2,1)S(1)} %bitcast.12, bf16[1728,1024]{1,0:T(8,128)(2,1)S(1)} %bitcast.13), custom_call_target="tpu_custom_call" | custom-call | flops 4000000000 | bytes 8388608 | tf_op jit(solution)/shard_map/pallas_call | solution.py:82
  17.4 3.5 %collective-permute-start = (f32[64,128]{1,0:T(8,128)S(1)}, f32[64,128]{1,0:T(8,128)S(1)}, u32[]{:S(2)}, u32[]{:S(2)}) collective-permute-start(f32[64,128]{1,0:T(8,128)S(1)} %get-tuple-element.15), channel_id=1, source_target_pairs={{0,16},{16,32},{32,48},{48,64},{64,80},{80,96},{96,112},{112,128},... | collective-permute-start | bytes 98312 | tf_op jit(solution)/shard_map/ppermute | solution.py:95
  21.0 1.0 %collective-permute-done.earlier_ref = f32[64,128]{1,0:T(8,128)S(1)} collective-permute-done((f32[64,128]{1,0:T(8,128)S(1)}, f32[64,128]{1,0:T(8,128)S(1)}, u32[]{:S(2)}, u32[]{:S(2)}) %collective-permute-start) | collective-permute-done | bytes 32800 | tf_op jit(solution)/shard_map/ppermute | solution.py:95
  22.0 10.7 %all_to_all.21 = bf16[16,64,128]{2,1,0:T(8,128)(2,1)S(1)} all-to-all(bf16[16,64,128]{2,1,0:T(8,128)(2,1)S(1)} %shard_map.66), channel_id=1, replica_groups=mesh['tm'=16,'chan'=16] {'chan'}, dimensions={0} | all-to-all | bytes 524288 | tf_op jit(solution)/shard_map/all_to_all | solution.py:259
  32.7 1.4 %shard_map.67 = (f32[64,128]{1,0:T(8,128)S(1)}, f32[64,128]{1,0:T(8,128)S(1)}) custom-call(bf16[1024,128]{1,0:T(8,128)(2,1)S(1)} %bitcast.11, bf16[1728,1024]{1,0:T(8,128)(2,1)S(1)} %bitcast.14, bf16[64,128]{1,0:T(8,128)(2,1)S(1)} %get-tuple-element.16.rest_0_), custom_call_target="tpu_custom_call" | custom-call | flops 4000000000 | bytes 8388608 | tf_op jit(solution)/shard_map/pallas_call | solution.py:82
  34.2 3.5 %collective-permute-start.3 = (f32[64,128]{1,0:T(8,128)S(1)}, f32[64,128]{1,0:T(8,128)S(1)}, u32[]{:S(2)}, u32[]{:S(2)}) collective-permute-start(f32[64,128]{1,0:T(8,128)S(1)} %get-tuple-element.18), channel_id=1, source_target_pairs={{0,20},{1,21},{2,22},{3,23},{4,16},{5,17},{6,18},{7,19},{8,28},{9,... | collective-permute-start | bytes 98312 | tf_op jit(solution)/shard_map/ppermute | solution.py:109
  37.7 1.5 %collective-permute-start.2 = (f32[64,128]{1,0:T(8,128)S(1)}, f32[64,128]{1,0:T(8,128)S(1)}, u32[]{:S(2)}, u32[]{:S(2)}) collective-permute-start(f32[64,128]{1,0:T(8,128)S(1)} %get-tuple-element.17.own_ref), channel_id=1, source_target_pairs={{0,4},{1,5},{2,6},{3,7},{4,0},{5,1},{6,2},{7,3},{8,12},{9,13},{10,... | collective-permute-start | bytes 98312 | tf_op jit(solution)/shard_map/ppermute | solution.py:99
  39.2 0.0 collective-permute-start.1
  39.2 1.3 %collective-permute-done.3.earlier_too_ref = f32[64,128]{1,0:T(8,128)S(1)} collective-permute-done((f32[64,128]{1,0:T(8,128)S(1)}, f32[64,128]{1,0:T(8,128)S(1)}, u32[]{:S(2)}, u32[]{:S(2)}) %collective-permute-start.3) | collective-permute-done | bytes 32800 | tf_op jit(solution)/shard_map/ppermute | solution.py:109
  40.5 1.5 %collective-permute-start.4 = (bf16[27,64,256]{2,1,0:T(8,128)(2,1)S(1)}, bf16[27,64,256]{2,1,0:T(8,128)(2,1)S(1)}, u32[]{:S(2)}, u32[]{:S(2)}) collective-permute-start(bf16[27,64,256]{2,1,0:T(8,128)(2,1)S(1)} %copy-done), channel_id=1, source_target_pairs={{0,4},{1,5},{2,6},{3,7},{4,0},{5,1},{6,2},{7,3},{8,12},{9,13},{10,... | collective-permute-start | bytes 2654216 | tf_op jit(solution)/shard_map/ppermute | solution.py:99
  42.0 0.0 collective-permute-done.2.own_too_ref
  42.1 0.0 collective-permute-done.1.earlier_ref
  42.1 0.2 shard_map.68
  42.2 0.0 copy-start.1
  42.3 15.0 %all_to_all.22 = bf16[8,80,128]{2,1,0:T(8,128)(2,1)S(1)} all-to-all(bf16[8,80,128]{2,1,0:T(8,128)(2,1)S(1)} %shard_map.68), channel_id=1, replica_groups={{0,32,64,96,128,160,192,224},{16,48,80,112,144,176,208,240},{1,33,65,97..., dimensions={0} | all-to-all | bytes 327680 | tf_op jit(solution)/shard_map/all_to_all | solution.py:275
  57.2 5.9 %all-gather = bf16[16,80,128]{2,1,0:T(8,128)(2,1)S(1)} all-gather(bf16[8,80,128]{2,1,0:T(8,128)(2,1)S(1)} %all_to_all.22), channel_id=2, replica_groups={{0,16},{32,48},{64,80},{96,112},{128,144},{160,176},{192,208},{224,240}..., dimensions={0}, use_global_device_ids=true | all-gather | bytes 491520 | tf_op jit(solution)/shard_map/all_gather | solution.py:276
  63.1 0.0 collective-permute-done.4.weight_too_ref
  63.1 2.8 %shard_map.69 = bf16[8,128,256]{2,1,0:T(8,128)(2,1)S(1)} custom-call(bf16[2,8,80,128]{3,2,1,0:T(8,128)(2,1)S(1)} %bitcast.10, bf16[1152,128]{1,0:T(8,128)(2,1)S(1)} %copy-done.2, bf16[27,64,256]{2,1,0:T(8,128)(2,1)S(1)} %copy-done, bf16[27,64,256]{2,1,0:T(8,128)(2,1)S(1)} %collective-permute-done.4.weight_too_ref), custom_call_target="tpu_custom_call" | custom-call | tf_op jit(solution)/shard_map/pallas_call | solution.py:280
  65.9 12.8 %all_to_all.23.parts_ref = bf16[8,128,256]{2,1,0:T(8,128)(2,1)S(1)} all-to-all(bf16[8,128,256]{2,1,0:T(8,128)(2,1)S(1)} %shard_map.69), channel_id=1, replica_groups={{4,5,6,7,8,9,10,11},{12,13,14,15,0,1,2,3},{20,21,22,23,24,25,26,27},{28..., dimensions={0} | all-to-all | bytes 1048576 | tf_op jit(solution)/shard_map/all_to_all | solution.py:289
  78.7 1.0 %shard_map.70 = bf16[2,32,512]{2,1,0:T(8,128)(2,1)} custom-call(bf16[8,128,256]{2,1,0:T(8,128)(2,1)S(1)} %all_to_all.23.parts_ref, bf16[512,512]{1,0:T(8,128)(2,1)S(1)} %copy-done.1), custom_call_target="tpu_custom_call" | custom-call | tf_op jit(solution)/shard_map/pallas_call | solution.py:290
  (10 shorter events, 0.0 us)
Async XLA Ops:
  0.0 0.8 copy-start.5
  0.8 15.2 %copy-start.3 = (bf16[64,27,1024]{2,0,1:T(8,128)(2,1)S(1)}, bf16[64,27,1024]{2,0,1:T(8,128)(2,1)}, u32[]{:S(2)}) copy-start(bf16[64,27,1024]{2,0,1:T(8,128)(2,1)} %param.7) | copy-start | bytes 10616836
  17.4 4.6 %collective-permute-start = (f32[64,128]{1,0:T(8,128)S(1)}, f32[64,128]{1,0:T(8,128)S(1)}, u32[]{:S(2)}, u32[]{:S(2)}) collective-permute-start(f32[64,128]{1,0:T(8,128)S(1)} %get-tuple-element.15), channel_id=1, source_target_pairs={{0,16},{16,32},{32,48},{48,64},{64,80},{80,96},{96,112},{112,128},... | collective-permute-start | bytes 98312 | tf_op jit(solution)/shard_map/ppermute | solution.py:95
  22.0 10.8 %copy-start.4 = (bf16[64,27,1024]{2,0,1:T(8,128)(2,1)S(1)}, bf16[64,27,1024]{2,0,1:T(8,128)(2,1)}, u32[]{:S(2)}) copy-start(bf16[64,27,1024]{2,0,1:T(8,128)(2,1)} %param.8) | copy-start | bytes 10616836
  32.7 7.8 %copy-start = (bf16[27,64,256]{2,1,0:T(8,128)(2,1)S(1)}, bf16[27,64,256]{2,1,0:T(8,128)(2,1)}, u32[]{:S(2)}) copy-start(bf16[27,64,256]{2,1,0:T(8,128)(2,1)} %weight_ref.1) | copy-start | bytes 2654212
  34.2 6.4 %collective-permute-start.3 = (f32[64,128]{1,0:T(8,128)S(1)}, f32[64,128]{1,0:T(8,128)S(1)}, u32[]{:S(2)}, u32[]{:S(2)}) collective-permute-start(f32[64,128]{1,0:T(8,128)S(1)} %get-tuple-element.18), channel_id=1, source_target_pairs={{0,20},{1,21},{2,22},{3,23},{4,16},{5,17},{6,18},{7,19},{8,28},{9,... | collective-permute-start | bytes 98312 | tf_op jit(solution)/shard_map/ppermute | solution.py:109
  37.7 25.4 %copy-start.2 = (bf16[1152,128]{1,0:T(8,128)(2,1)S(1)}, bf16[1152,128]{1,0:T(8,128)(2,1)}, u32[]{:S(2)}) copy-start(bf16[1152,128]{1,0:T(8,128)(2,1)} %constant.4.clone.move_ref) | copy-start | bytes 884740
  37.7 4.4 %collective-permute-start.2 = (f32[64,128]{1,0:T(8,128)S(1)}, f32[64,128]{1,0:T(8,128)S(1)}, u32[]{:S(2)}, u32[]{:S(2)}) collective-permute-start(f32[64,128]{1,0:T(8,128)S(1)} %get-tuple-element.17.own_ref), channel_id=1, source_target_pairs={{0,4},{1,5},{2,6},{3,7},{4,0},{5,1},{6,2},{7,3},{8,12},{9,13},{10,... | collective-permute-start | bytes 98312 | tf_op jit(solution)/shard_map/ppermute | solution.py:99
  39.2 2.8 %collective-permute-start.1 = (f32[64,128]{1,0:T(8,128)S(1)}, f32[64,128]{1,0:T(8,128)S(1)}, u32[]{:S(2)}, u32[]{:S(2)}) collective-permute-start(f32[64,128]{1,0:T(8,128)S(1)} %get-tuple-element.18), channel_id=1, source_target_pairs={{0,16},{16,32},{32,48},{48,64},{64,80},{80,96},{96,112},{112,128},... | collective-permute-start | bytes 98312 | tf_op jit(solution)/shard_map/ppermute | solution.py:95
  40.5 22.6 %collective-permute-start.4 = (bf16[27,64,256]{2,1,0:T(8,128)(2,1)S(1)}, bf16[27,64,256]{2,1,0:T(8,128)(2,1)S(1)}, u32[]{:S(2)}, u32[]{:S(2)}) collective-permute-start(bf16[27,64,256]{2,1,0:T(8,128)(2,1)S(1)} %copy-done), channel_id=1, source_target_pairs={{0,4},{1,5},{2,6},{3,7},{4,0},{5,1},{6,2},{7,3},{8,12},{9,13},{10,... | collective-permute-start | bytes 2654216 | tf_op jit(solution)/shard_map/ppermute | solution.py:99
  42.2 36.5 %copy-start.1 = (bf16[512,512]{1,0:T(8,128)(2,1)S(1)}, bf16[512,512]{1,0:T(8,128)(2,1)}, u32[]{:S(2)}) copy-start(bf16[512,512]{1,0:T(8,128)(2,1)} %constant.5.clone.spread_ref) | copy-start | bytes 1572868

commit v5 on v4

--- a/solution.py
+++ b/solution.py
@@ -47,8 +47,7 @@
 
 
 def start_kernel(latent_ref, places_ref, copies_ref):
-    cells = [latent_ref[t, r] for r in range(ROWS) for t in range(FRAMES)]
-    places = jnp.concatenate(cells, axis=0).astype(F32).T.astype(BF16)
+    places = latent_ref[...].astype(F32).T.astype(BF16)
     places_ref[...] = places
     for i in range(copies_ref.shape[0]):
         copies_ref[i] = places
@@ -149,18 +148,25 @@
     channels = all_ref.shape[3]
     inner = jnp.where(middle(), 1.0, 0.0).astype(BF16)
     for row in range(0, BANDS * BAND + 2, 2):
-        places = []
-        for r in (row, row + 1):
-            cells = [
-                all_ref[i % 2, i // 2, r * CELL : (r + 1) * CELL].astype(F32)
-                for i in range(count)
-            ]
-            places.append(jnp.concatenate(cells, axis=0))
+        cells = [
+            all_ref[i % 2, i // 2, row * CELL : (row + 2) * CELL].astype(F32)
+            for i in range(count)
+        ]
+        places = [
+            jnp.concatenate([cell[j * CELL : (j + 1) * CELL] for cell in cells], axis=0)
+            for j in range(2)
+        ]
         pair = jnp.concatenate(places, axis=1).astype(BF16)
-        result = jnp.dot(move_ref[...], pair, preferred_element_type=F32).astype(BF16)
+        result = jnp.dot(move_ref[...], pair, preferred_element_type=F32)
+        blocks = [result[k * LANES : (k + 1) * LANES] for k in range(6)]
+        blocks = [
+            jnp.concatenate([block[:COLS], block[:COLS], block[: LANES - CELL]], axis=0)
+            for block in blocks[3:]
+        ] + blocks
         for k in range(9):
+            block = blocks[k].astype(BF16)
             for j in range(2):
-                piece = result[k * LANES : (k + 1) * LANES, j * channels : (j + 1) * channels]
+                piece = block[:, j * channels : (j + 1) * channels]
                 for band in range(BANDS):
                     at = row + j - band * BAND
                     if 0 <= at < BAND + 2:
@@ -192,7 +198,7 @@
     place = np.arange(LANES)
     frame, col = place // COLS, place % COLS
     blocks = []
-    for frame_off in range(3):
+    for frame_off in (1, 2):
         for col_off in range(3):
             target = col + col_off - 1
             source = np.maximum(frame + frame_off - 2, 0) * COLS + target
@@ -249,7 +255,7 @@
             jax.ShapeDtypeStruct((channels_on,) + shape, BF16),
         ),
         **hint(8),
-    )(jnp.transpose(latent, (0, 2, 3, 1)))
+    )(jnp.transpose(latent, (2, 0, 3, 1)).reshape(LANES, channels))
     whole = lax.all_to_all(copies, "chan", 0, 0, tiled=True).reshape(-1, LANES)
 
     own, later = block_conv(whole, taps(conv_first), channels)

time: 80.2 us -> 79.9 us (level)
  no operation moved by 1% of the time
where the time goes in v5:
time: 79.9 us; the launch traced here: 79.5 us
  blocking collectives  59.5 us (74%)
  starting transfers between devices  10.1 us (13%)
  Pallas kernels  6.66 us (8%)
  waiting for transfers between devices  2.34 us (3%)
    all_to_all x2, blocking collectives, on_device(): whole = lax.all_to_all(copies, 'chan', 0, 0, tiled=True).reshape(-1, LANES)  25.8 us
    all_to_all x1, blocking collectives, on_device(): lax.all_to_all(copies, 'tm', 0, 0, tiled=True, axis_index_groups=along)  15 us
    all_to_all x1, blocking collectives, on_device(): lax.all_to_all(partial, 'chan', 0, 0, tiled=True, axis_index_groups=groups)  12.8 us
    all_gather x1, blocking collectives, on_device(): frames = lax.all_gather(frames, 'tm', axis_index_groups=cores)  5.87 us
    ppermute x2, starting transfers between devices, shifted_on(): lax.ppermute(later, 'tm', [(i, next_frames(i)) for i in range(lax.axis_si...  3.56 us
    ppermute x1, starting transfers between devices, shifted_and_swapped(): return lax.ppermute(later, ('tm', 'chan'), pairs)  3.52 us
    ppermute x2, starting transfers between devices, swapped(): lax.ppermute(value, 'chan', [(c, c ^ PAIR) for c in range(lax.axis_size('...  3.04 us
    pallas_call x2, Pallas kernels, block_conv(): pl.pallas_call(block_kernel, out_shape=(shape, shape), compiler_params=pl...  2.85 us
  transfers between devices with their start and end apart: 5, of which 2 were waited for; matrix products, arithmetic and copies ran while one was open for 0% of the time, Pallas kernels for 0%

profile of v5, /device:TPU:1, one launch (start us, length us, event | category | flops | bytes accessed | tf_op | source)
XLA Modules:
  0.0 79.5 jit_solution(13495862544997721896)
XLA Ops:
  0.0 0.8 copy.8
  0.8 0.0 copy-start.3
  0.8 0.1 shard_map.64
  0.9 15.1 %all_to_all.20 = bf16[16,64,128]{2,1,0:T(8,128)(2,1)S(1)} all-to-all(bf16[16,64,128]{2,1,0:T(8,128)(2,1)S(1)} %get-tuple-element.13), channel_id=1, replica_groups=mesh['tm'=16,'chan'=16] {'chan'}, dimensions={0} | all-to-all | bytes 524288 | tf_op jit(solution)/shard_map/all_to_all | solution.py:259
  16.0 1.4 %shard_map.65 = (f32[64,128]{1,0:T(8,128)S(1)}, f32[64,128]{1,0:T(8,128)S(1)}) custom-call(bf16[1024,128]{1,0:T(8,128)(2,1)S(1)} %bitcast.13, bf16[1728,1024]{1,0:T(8,128)(2,1)S(1)} %bitcast.15), custom_call_target="tpu_custom_call" | custom-call | flops 4000000000 | bytes 8388608 | tf_op jit(solution)/shard_map/pallas_call | solution.py:81
  17.4 3.6 %collective-permute-start = (f32[64,128]{1,0:T(8,128)S(1)}, f32[64,128]{1,0:T(8,128)S(1)}, u32[]{:S(2)}, u32[]{:S(2)}) collective-permute-start(f32[64,128]{1,0:T(8,128)S(1)} %get-tuple-element.15), channel_id=1, source_target_pairs={{0,16},{16,32},{32,48},{48,64},{64,80},{80,96},{96,112},{112,128},... | collective-permute-start | bytes 98312 | tf_op jit(solution)/shard_map/ppermute | solution.py:94
  21.0 1.0 %collective-permute-done.earlier_ref = f32[64,128]{1,0:T(8,128)S(1)} collective-permute-done((f32[64,128]{1,0:T(8,128)S(1)}, f32[64,128]{1,0:T(8,128)S(1)}, u32[]{:S(2)}, u32[]{:S(2)}) %collective-permute-start) | collective-permute-done | bytes 32800 | tf_op jit(solution)/shard_map/ppermute | solution.py:94
  22.0 10.7 %all_to_all.21 = bf16[16,64,128]{2,1,0:T(8,128)(2,1)S(1)} all-to-all(bf16[16,64,128]{2,1,0:T(8,128)(2,1)S(1)} %shard_map.66), channel_id=1, replica_groups=mesh['tm'=16,'chan'=16] {'chan'}, dimensions={0} | all-to-all | bytes 524288 | tf_op jit(solution)/shard_map/all_to_all | solution.py:265
  32.8 1.4 %shard_map.67 = (f32[64,128]{1,0:T(8,128)S(1)}, f32[64,128]{1,0:T(8,128)S(1)}) custom-call(bf16[1024,128]{1,0:T(8,128)(2,1)S(1)} %bitcast.12, bf16[1728,1024]{1,0:T(8,128)(2,1)S(1)} %bitcast.16, bf16[64,128]{1,0:T(8,128)(2,1)S(1)} %get-tuple-element.16.rest_0_), custom_call_target="tpu_custom_call" | custom-call | flops 4000000000 | bytes 8388608 | tf_op jit(solution)/shard_map/pallas_call | solution.py:81
  34.2 3.5 %collective-permute-start.3 = (f32[64,128]{1,0:T(8,128)S(1)}, f32[64,128]{1,0:T(8,128)S(1)}, u32[]{:S(2)}, u32[]{:S(2)}) collective-permute-start(f32[64,128]{1,0:T(8,128)S(1)} %get-tuple-element.18), channel_id=1, source_target_pairs={{0,20},{1,21},{2,22},{3,23},{4,16},{5,17},{6,18},{7,19},{8,28},{9,... | collective-permute-start | bytes 98312 | tf_op jit(solution)/shard_map/ppermute | solution.py:108
  37.7 1.5 %collective-permute-start.2 = (f32[64,128]{1,0:T(8,128)S(1)}, f32[64,128]{1,0:T(8,128)S(1)}, u32[]{:S(2)}, u32[]{:S(2)}) collective-permute-start(f32[64,128]{1,0:T(8,128)S(1)} %get-tuple-element.17.own_ref), channel_id=1, source_target_pairs={{0,4},{1,5},{2,6},{3,7},{4,0},{5,1},{6,2},{7,3},{8,12},{9,13},{10,... | collective-permute-start | bytes 98312 | tf_op jit(solution)/shard_map/ppermute | solution.py:98
  39.3 0.0 collective-permute-start.1
  39.3 1.3 %collective-permute-done.3.earlier_too_ref = f32[64,128]{1,0:T(8,128)S(1)} collective-permute-done((f32[64,128]{1,0:T(8,128)S(1)}, f32[64,128]{1,0:T(8,128)S(1)}, u32[]{:S(2)}, u32[]{:S(2)}) %collective-permute-start.3) | collective-permute-done | bytes 32800 | tf_op jit(solution)/shard_map/ppermute | solution.py:108
  40.6 1.5 %collective-permute-start.4 = (bf16[27,64,256]{2,1,0:T(8,128)(2,1)S(1)}, bf16[27,64,256]{2,1,0:T(8,128)(2,1)S(1)}, u32[]{:S(2)}, u32[]{:S(2)}) collective-permute-start(bf16[27,64,256]{2,1,0:T(8,128)(2,1)S(1)} %copy-done), channel_id=1, source_target_pairs={{0,4},{1,5},{2,6},{3,7},{4,0},{5,1},{6,2},{7,3},{8,12},{9,13},{10,... | collective-permute-start | bytes 2654216 | tf_op jit(solution)/shard_map/ppermute | solution.py:98
  42.1 0.0 collective-permute-done.2.own_too_ref
  42.1 0.0 collective-permute-done.1.earlier_ref
  42.1 0.2 shard_map.68
  42.3 0.0 copy-start.1
  42.3 15.0 %all_to_all.22 = bf16[8,80,128]{2,1,0:T(8,128)(2,1)S(1)} all-to-all(bf16[8,80,128]{2,1,0:T(8,128)(2,1)S(1)} %shard_map.68), channel_id=1, replica_groups={{0,32,64,96,128,160,192,224},{16,48,80,112,144,176,208,240},{1,33,65,97..., dimensions={0} | all-to-all | bytes 327680 | tf_op jit(solution)/shard_map/all_to_all | solution.py:281
  57.3 5.9 %all-gather = bf16[16,80,128]{2,1,0:T(8,128)(2,1)S(1)} all-gather(bf16[8,80,128]{2,1,0:T(8,128)(2,1)S(1)} %all_to_all.22), channel_id=2, replica_groups={{0,16},{32,48},{64,80},{96,112},{128,144},{160,176},{192,208},{224,240}..., dimensions={0}, use_global_device_ids=true | all-gather | bytes 491520 | tf_op jit(solution)/shard_map/all_gather | solution.py:282
  63.1 0.0 collective-permute-done.4.weight_too_ref
  63.1 2.6 %shard_map.69 = bf16[8,128,256]{2,1,0:T(8,128)(2,1)S(1)} custom-call(bf16[2,8,80,128]{3,2,1,0:T(8,128)(2,1)S(1)} %bitcast.11, bf16[768,128]{1,0:T(8,128)(2,1)S(1)} %copy-done.2, bf16[27,64,256]{2,1,0:T(8,128)(2,1)S(1)} %copy-done, bf16[27,64,256]{2,1,0:T(8,128)(2,1)S(1)} %collective-permute-done.4.weight_too_ref), custom_call_target="tpu_custom_call" | custom-call | tf_op jit(solution)/shard_map/pallas_call | solution.py:286
  65.7 12.8 %all_to_all.23.parts_ref = bf16[8,128,256]{2,1,0:T(8,128)(2,1)S(1)} all-to-all(bf16[8,128,256]{2,1,0:T(8,128)(2,1)S(1)} %shard_map.69), channel_id=1, replica_groups={{4,5,6,7,8,9,10,11},{12,13,14,15,0,1,2,3},{20,21,22,23,24,25,26,27},{28..., dimensions={0} | all-to-all | bytes 1048576 | tf_op jit(solution)/shard_map/all_to_all | solution.py:295
  78.5 1.0 %shard_map.70 = bf16[2,32,512]{2,1,0:T(8,128)(2,1)} custom-call(bf16[8,128,256]{2,1,0:T(8,128)(2,1)S(1)} %all_to_all.23.parts_ref, bf16[512,512]{1,0:T(8,128)(2,1)S(1)} %copy-done.1), custom_call_target="tpu_custom_call" | custom-call | tf_op jit(solution)/shard_map/pallas_call | solution.py:296
  (9 shorter events, 0.0 us)
Async XLA Ops:
  0.8 15.2 %copy-start.3 = (bf16[64,27,1024]{2,0,1:T(8,128)(2,1)S(1)}, bf16[64,27,1024]{2,0,1:T(8,128)(2,1)}, u32[]{:S(2)}) copy-start(bf16[64,27,1024]{2,0,1:T(8,128)(2,1)} %param.7) | copy-start | bytes 10616836
  17.4 4.6 %collective-permute-start = (f32[64,128]{1,0:T(8,128)S(1)}, f32[64,128]{1,0:T(8,128)S(1)}, u32[]{:S(2)}, u32[]{:S(2)}) collective-permute-start(f32[64,128]{1,0:T(8,128)S(1)} %get-tuple-element.15), channel_id=1, source_target_pairs={{0,16},{16,32},{32,48},{48,64},{64,80},{80,96},{96,112},{112,128},... | collective-permute-start | bytes 98312 | tf_op jit(solution)/shard_map/ppermute | solution.py:94
  22.0 10.8 %copy-start.4 = (bf16[64,27,1024]{2,0,1:T(8,128)(2,1)S(1)}, bf16[64,27,1024]{2,0,1:T(8,128)(2,1)}, u32[]{:S(2)}) copy-start(bf16[64,27,1024]{2,0,1:T(8,128)(2,1)} %param.8) | copy-start | bytes 10616836
  32.8 7.8 %copy-start = (bf16[27,64,256]{2,1,0:T(8,128)(2,1)S(1)}, bf16[27,64,256]{2,1,0:T(8,128)(2,1)}, u32[]{:S(2)}) copy-start(bf16[27,64,256]{2,1,0:T(8,128)(2,1)} %weight_ref.1) | copy-start | bytes 2654212
  34.2 6.4 %collective-permute-start.3 = (f32[64,128]{1,0:T(8,128)S(1)}, f32[64,128]{1,0:T(8,128)S(1)}, u32[]{:S(2)}, u32[]{:S(2)}) collective-permute-start(f32[64,128]{1,0:T(8,128)S(1)} %get-tuple-element.18), channel_id=1, source_target_pairs={{0,20},{1,21},{2,22},{3,23},{4,16},{5,17},{6,18},{7,19},{8,28},{9,... | collective-permute-start | bytes 98312 | tf_op jit(solution)/shard_map/ppermute | solution.py:108
  37.7 25.4 %copy-start.2 = (bf16[768,128]{1,0:T(8,128)(2,1)S(1)}, bf16[768,128]{1,0:T(8,128)(2,1)}, u32[]{:S(2)}) copy-start(bf16[768,128]{1,0:T(8,128)(2,1)} %constant.4.clone.move_ref) | copy-start | bytes 589828
  37.7 4.4 %collective-permute-start.2 = (f32[64,128]{1,0:T(8,128)S(1)}, f32[64,128]{1,0:T(8,128)S(1)}, u32[]{:S(2)}, u32[]{:S(2)}) collective-permute-start(f32[64,128]{1,0:T(8,128)S(1)} %get-tuple-element.17.own_ref), channel_id=1, source_target_pairs={{0,4},{1,5},{2,6},{3,7},{4,0},{5,1},{6,2},{7,3},{8,12},{9,13},{10,... | collective-permute-start | bytes 98312 | tf_op jit(solution)/shard_map/ppermute | solution.py:98
  39.3 2.8 %collective-permute-start.1 = (f32[64,128]{1,0:T(8,128)S(1)}, f32[64,128]{1,0:T(8,128)S(1)}, u32[]{:S(2)}, u32[]{:S(2)}) collective-permute-start(f32[64,128]{1,0:T(8,128)S(1)} %get-tuple-element.18), channel_id=1, source_target_pairs={{0,16},{16,32},{32,48},{48,64},{64,80},{80,96},{96,112},{112,128},... | collective-permute-start | bytes 98312 | tf_op jit(solution)/shard_map/ppermute | solution.py:94
  40.6 22.6 %collective-permute-start.4 = (bf16[27,64,256]{2,1,0:T(8,128)(2,1)S(1)}, bf16[27,64,256]{2,1,0:T(8,128)(2,1)S(1)}, u32[]{:S(2)}, u32[]{:S(2)}) collective-permute-start(bf16[27,64,256]{2,1,0:T(8,128)(2,1)S(1)} %copy-done), channel_id=1, source_target_pairs={{0,4},{1,5},{2,6},{3,7},{4,0},{5,1},{6,2},{7,3},{8,12},{9,13},{10,... | collective-permute-start | bytes 2654216 | tf_op jit(solution)/shard_map/ppermute | solution.py:98
  42.3 36.2 %copy-start.1 = (bf16[512,512]{1,0:T(8,128)(2,1)S(1)}, bf16[512,512]{1,0:T(8,128)(2,1)}, u32[]{:S(2)}) copy-start(bf16[512,512]{1,0:T(8,128)(2,1)} %constant.5.clone.spread_ref) | copy-start | bytes 1572868

commit v6 on v5

--- a/solution.py
+++ b/solution.py
@@ -143,15 +143,16 @@
     }
 
 
-def upsample_kernel(all_ref, move_ref, weight_ref, weight_too_ref, out_ref, moved):
-    count = 2 * all_ref.shape[1]
-    channels = all_ref.shape[3]
+def upsample_kernel(here_ref, there_ref, move_ref, weight_ref, weight_too_ref, out_ref, moved):
+    chips, _, channels = here_ref.shape
+    low = lax.axis_index("tm") % 2 == 0
     inner = jnp.where(middle(), 1.0, 0.0).astype(BF16)
     for row in range(0, BANDS * BAND + 2, 2):
-        cells = [
-            all_ref[i % 2, i // 2, row * CELL : (row + 2) * CELL].astype(F32)
-            for i in range(count)
-        ]
+        cells = []
+        for i in range(chips):
+            here = here_ref[i, row * CELL : (row + 2) * CELL].astype(F32)
+            there = there_ref[i, row * CELL : (row + 2) * CELL].astype(F32)
+            cells += [jnp.where(low, here, there), jnp.where(low, there, here)]
         places = [
             jnp.concatenate([cell[j * CELL : (j + 1) * CELL] for cell in cells], axis=0)
             for j in range(2)
@@ -277,9 +278,8 @@
         **hint(8),
     )(own, earlier, own_too, earlier_too)
     along = [list(range(core, frames_on, 2)) for core in range(2)]
-    cores = [[i, i + 1] for i in range(0, frames_on, 2)]
     frames = lax.all_to_all(copies, "tm", 0, 0, tiled=True, axis_index_groups=along)
-    frames = lax.all_gather(frames, "tm", axis_index_groups=cores)
+    frames_too = lax.ppermute(frames, "tm", [(i, i ^ 1) for i in range(frames_on)])
 
     outs = conv_upsample.shape[2]
     rows_here = BANDS * BAND
@@ -288,7 +288,7 @@
         out_shape=jax.ShapeDtypeStruct((rows_here, LANES, outs), BF16),
         scratch_shapes=[pltpu.VMEM((9, BANDS, (BAND + 2) * LANES, 2 * channels), BF16)],
         compiler_params=pltpu.CompilerParams(vmem_limit_bytes=32 * MIB),
-    )(frames, moves(), conv_upsample, other)
+    )(frames, frames_too, moves(), conv_upsample, other)
     groups = [
         [place * PAIR + c for place in pair for c in range(PAIR)] for pair in ((1, 2), (3, 0))
     ]

time: 79.9 us -> 79.4 us (level)
  blocking collectives: 59.5 us -> 53.6 us
  starting transfers between devices: 10.1 us -> 14.3 us
  waiting for transfers between devices: 2.34 us -> 3.37 us
    all_gather x1 -> x0, blocking collectives: 5.87 us -> none  [on_device(): frames = lax.all_gather(frames, 'tm', axis_index_groups=cores)]
    ppermute x0 -> x1, starting transfers between devices: none -> 4.2 us  [on_device(): lax.ppermute(frames, 'tm', [(i, i ^ 1) for i in range(frames_on)])]
    ppermute x0 -> x1, waiting for transfers between devices: none -> 1.03 us  [on_device(): lax.ppermute(frames, 'tm', [(i, i ^ 1) for i in range(frames_on)])]
  transfers between devices with their start and end apart: 5 -> 6, of which waited for: 2 -> 3; matrix products, arithmetic and copies ran while one was open for 0% -> 0% of each run, Pallas kernels for 0% -> 0%
where the time goes in v6:
time: 79.4 us; the launch traced here: 78.8 us
  blocking collectives  53.6 us (68%)
  starting transfers between devices  14.3 us (18%)
  Pallas kernels  6.67 us (8%)
  waiting for transfers between devices  3.37 us (4%)
    all_to_all x2, blocking collectives, on_device(): whole = lax.all_to_all(copies, 'chan', 0, 0, tiled=True).reshape(-1, LANES)  25.8 us
    all_to_all x1, blocking collectives, on_device(): lax.all_to_all(copies, 'tm', 0, 0, tiled=True, axis_index_groups=along)  15 us
    all_to_all x1, blocking collectives, on_device(): lax.all_to_all(partial, 'chan', 0, 0, tiled=True, axis_index_groups=groups)  12.8 us
    ppermute x1, starting transfers between devices, on_device(): lax.ppermute(frames, 'tm', [(i, i ^ 1) for i in range(frames_on)])  4.2 us
    ppermute x2, starting transfers between devices, shifted_on(): lax.ppermute(later, 'tm', [(i, next_frames(i)) for i in range(lax.axis_si...  3.56 us
    ppermute x1, starting transfers between devices, shifted_and_swapped(): return lax.ppermute(later, ('tm', 'chan'), pairs)  3.52 us
    ppermute x2, starting transfers between devices, swapped(): lax.ppermute(value, 'chan', [(c, c ^ PAIR) for c in range(lax.axis_size('...  3.04 us
    pallas_call x2, Pallas kernels, block_conv(): pl.pallas_call(block_kernel, out_shape=(shape, shape), compiler_params=pl...  2.85 us
  transfers between devices with their start and end apart: 6, of which 3 were waited for; matrix products, arithmetic and copies ran while one was open for 0% of the time, Pallas kernels for 0%

profile of v6, /device:TPU:1, one launch (start us, length us, event | category | flops | bytes accessed | tf_op | source)
XLA Modules:
  0.0 78.8 jit_solution(5201207873709645046)
XLA Ops:
  0.0 0.8 copy.7
  0.8 0.0 copy-start.3
  0.8 0.1 shard_map.64
  0.9 15.1 %all_to_all.20 = bf16[16,64,128]{2,1,0:T(8,128)(2,1)S(1)} all-to-all(bf16[16,64,128]{2,1,0:T(8,128)(2,1)S(1)} %get-tuple-element.13), channel_id=1, replica_groups=mesh['tm'=16,'chan'=16] {'chan'}, dimensions={0} | all-to-all | bytes 524288 | tf_op jit(solution)/shard_map/all_to_all | solution.py:260
  16.0 1.4 %shard_map.65 = (f32[64,128]{1,0:T(8,128)S(1)}, f32[64,128]{1,0:T(8,128)S(1)}) custom-call(bf16[1024,128]{1,0:T(8,128)(2,1)S(1)} %bitcast.11, bf16[1728,1024]{1,0:T(8,128)(2,1)S(1)} %bitcast.13), custom_call_target="tpu_custom_call" | custom-call | flops 4000000000 | bytes 8388608 | tf_op jit(solution)/shard_map/pallas_call | solution.py:81
  17.4 3.6 %collective-permute-start = (f32[64,128]{1,0:T(8,128)S(1)}, f32[64,128]{1,0:T(8,128)S(1)}, u32[]{:S(2)}, u32[]{:S(2)}) collective-permute-start(f32[64,128]{1,0:T(8,128)S(1)} %get-tuple-element.15), channel_id=1, source_target_pairs={{0,16},{16,32},{32,48},{48,64},{64,80},{80,96},{96,112},{112,128},... | collective-permute-start | bytes 98312 | tf_op jit(solution)/shard_map/ppermute | solution.py:94
  21.0 1.0 %collective-permute-done.earlier_ref = f32[64,128]{1,0:T(8,128)S(1)} collective-permute-done((f32[64,128]{1,0:T(8,128)S(1)}, f32[64,128]{1,0:T(8,128)S(1)}, u32[]{:S(2)}, u32[]{:S(2)}) %collective-permute-start) | collective-permute-done | bytes 32800 | tf_op jit(solution)/shard_map/ppermute | solution.py:94
  22.0 10.7 %all_to_all.21 = bf16[16,64,128]{2,1,0:T(8,128)(2,1)S(1)} all-to-all(bf16[16,64,128]{2,1,0:T(8,128)(2,1)S(1)} %shard_map.66), channel_id=1, replica_groups=mesh['tm'=16,'chan'=16] {'chan'}, dimensions={0} | all-to-all | bytes 524288 | tf_op jit(solution)/shard_map/all_to_all | solution.py:266
  32.8 1.4 %shard_map.67 = (f32[64,128]{1,0:T(8,128)S(1)}, f32[64,128]{1,0:T(8,128)S(1)}) custom-call(bf16[1024,128]{1,0:T(8,128)(2,1)S(1)} %bitcast.10, bf16[1728,1024]{1,0:T(8,128)(2,1)S(1)} %bitcast.14, bf16[64,128]{1,0:T(8,128)(2,1)S(1)} %get-tuple-element.16.rest_0_), custom_call_target="tpu_custom_call" | custom-call | flops 4000000000 | bytes 8388608 | tf_op jit(solution)/shard_map/pallas_call | solution.py:81
  34.2 3.5 %collective-permute-start.3 = (f32[64,128]{1,0:T(8,128)S(1)}, f32[64,128]{1,0:T(8,128)S(1)}, u32[]{:S(2)}, u32[]{:S(2)}) collective-permute-start(f32[64,128]{1,0:T(8,128)S(1)} %get-tuple-element.18), channel_id=1, source_target_pairs={{0,20},{1,21},{2,22},{3,23},{4,16},{5,17},{6,18},{7,19},{8,28},{9,... | collective-permute-start | bytes 98312 | tf_op jit(solution)/shard_map/ppermute | solution.py:108
  37.7 1.5 %collective-permute-start.2 = (f32[64,128]{1,0:T(8,128)S(1)}, f32[64,128]{1,0:T(8,128)S(1)}, u32[]{:S(2)}, u32[]{:S(2)}) collective-permute-start(f32[64,128]{1,0:T(8,128)S(1)} %get-tuple-element.17.own_ref), channel_id=1, source_target_pairs={{0,4},{1,5},{2,6},{3,7},{4,0},{5,1},{6,2},{7,3},{8,12},{9,13},{10,... | collective-permute-start | bytes 98312 | tf_op jit(solution)/shard_map/ppermute | solution.py:98
  39.3 0.0 collective-permute-start.1
  39.3 1.3 %collective-permute-done.3.earlier_too_ref = f32[64,128]{1,0:T(8,128)S(1)} collective-permute-done((f32[64,128]{1,0:T(8,128)S(1)}, f32[64,128]{1,0:T(8,128)S(1)}, u32[]{:S(2)}, u32[]{:S(2)}) %collective-permute-start.3) | collective-permute-done | bytes 32800 | tf_op jit(solution)/shard_map/ppermute | solution.py:108
  40.6 1.5 %collective-permute-start.5 = (bf16[27,64,256]{2,1,0:T(8,128)(2,1)S(1)}, bf16[27,64,256]{2,1,0:T(8,128)(2,1)S(1)}, u32[]{:S(2)}, u32[]{:S(2)}) collective-permute-start(bf16[27,64,256]{2,1,0:T(8,128)(2,1)S(1)} %copy-done), channel_id=1, source_target_pairs={{0,4},{1,5},{2,6},{3,7},{4,0},{5,1},{6,2},{7,3},{8,12},{9,13},{10,... | collective-permute-start | bytes 2654216 | tf_op jit(solution)/shard_map/ppermute | solution.py:98
  42.1 0.0 collective-permute-done.2.own_too_ref
  42.1 0.0 collective-permute-done.1.earlier_ref
  42.1 0.2 shard_map.68
  42.3 0.0 copy-start.1
  42.3 15.0 %all_to_all.22.here_ref = bf16[8,80,128]{2,1,0:T(8,128)(2,1)S(1)} all-to-all(bf16[8,80,128]{2,1,0:T(8,128)(2,1)S(1)} %shard_map.68), channel_id=1, replica_groups={{0,32,64,96,128,160,192,224},{16,48,80,112,144,176,208,240},{1,33,65,97..., dimensions={0} | all-to-all | bytes 327680 | tf_op jit(solution)/shard_map/all_to_all | solution.py:281
  57.3 4.2 %collective-permute-start.4 = (bf16[8,80,128]{2,1,0:T(8,128)(2,1)S(1)}, bf16[8,80,128]{2,1,0:T(8,128)(2,1)S(1)}, u32[]{:S(2)}, u32[]{:S(2)}) collective-permute-start(bf16[8,80,128]{2,1,0:T(8,128)(2,1)S(1)} %all_to_all.22.here_ref), channel_id=1, source_target_pairs={{0,16},{16,0},{32,48},{48,32},{64,80},{80,64},{96,112},{112,96},{1... | collective-permute-start | bytes 491528 | tf_op jit(solution)/shard_map/ppermute | solution.py:282
  61.5 1.0 %collective-permute-done.4.there_ref = bf16[8,80,128]{2,1,0:T(8,128)(2,1)S(1)} collective-permute-done((bf16[8,80,128]{2,1,0:T(8,128)(2,1)S(1)}, bf16[8,80,128]{2,1,0:T(8,128)(2,1)S(1)}, u32[]{:S(2)}, u32[]{:S(2)}) %collective-permute-start.4) | collective-permute-done | bytes 163872 | tf_op jit(solution)/shard_map/ppermute | solution.py:282
  62.5 2.6 %shard_map.69 = bf16[8,128,256]{2,1,0:T(8,128)(2,1)S(1)} custom-call(bf16[8,80,128]{2,1,0:T(8,128)(2,1)S(1)} %all_to_all.22.here_ref, bf16[8,80,128]{2,1,0:T(8,128)(2,1)S(1)} %collective-permute-done.4.there_ref, bf16[768,128]{1,0:T(8,128)(2,1)S(1)} %copy-done.2, bf16[27,64,256]{2,1,0:T(8,128)(2,1)S(1)} %copy-done, ...), custom_call_target="tpu_custom_call" | custom-call | tf_op jit(solution)/shard_map/pallas_call | solution.py:286
  65.1 12.8 %all_to_all.23.parts_ref = bf16[8,128,256]{2,1,0:T(8,128)(2,1)S(1)} all-to-all(bf16[8,128,256]{2,1,0:T(8,128)(2,1)S(1)} %shard_map.69), channel_id=1, replica_groups={{4,5,6,7,8,9,10,11},{12,13,14,15,0,1,2,3},{20,21,22,23,24,25,26,27},{28..., dimensions={0} | all-to-all | bytes 1048576 | tf_op jit(solution)/shard_map/all_to_all | solution.py:295
  77.9 1.0 %shard_map.70 = bf16[2,32,512]{2,1,0:T(8,128)(2,1)} custom-call(bf16[8,128,256]{2,1,0:T(8,128)(2,1)S(1)} %all_to_all.23.parts_ref, bf16[512,512]{1,0:T(8,128)(2,1)S(1)} %copy-done.1), custom_call_target="tpu_custom_call" | custom-call | tf_op jit(solution)/shard_map/pallas_call | solution.py:296
  (10 shorter events, 0.0 us)
Async XLA Ops:
  0.8 15.2 %copy-start.3 = (bf16[64,27,1024]{2,0,1:T(8,128)(2,1)S(1)}, bf16[64,27,1024]{2,0,1:T(8,128)(2,1)}, u32[]{:S(2)}) copy-start(bf16[64,27,1024]{2,0,1:T(8,128)(2,1)} %param.7) | copy-start | bytes 10616836
  17.4 4.6 %collective-permute-start = (f32[64,128]{1,0:T(8,128)S(1)}, f32[64,128]{1,0:T(8,128)S(1)}, u32[]{:S(2)}, u32[]{:S(2)}) collective-permute-start(f32[64,128]{1,0:T(8,128)S(1)} %get-tuple-element.15), channel_id=1, source_target_pairs={{0,16},{16,32},{32,48},{48,64},{64,80},{80,96},{96,112},{112,128},... | collective-permute-start | bytes 98312 | tf_op jit(solution)/shard_map/ppermute | solution.py:94
  22.0 10.8 %copy-start.4 = (bf16[64,27,1024]{2,0,1:T(8,128)(2,1)S(1)}, bf16[64,27,1024]{2,0,1:T(8,128)(2,1)}, u32[]{:S(2)}) copy-start(bf16[64,27,1024]{2,0,1:T(8,128)(2,1)} %param.8) | copy-start | bytes 10616836
  32.8 7.8 %copy-start = (bf16[27,64,256]{2,1,0:T(8,128)(2,1)S(1)}, bf16[27,64,256]{2,1,0:T(8,128)(2,1)}, u32[]{:S(2)}) copy-start(bf16[27,64,256]{2,1,0:T(8,128)(2,1)} %weight_ref.1) | copy-start | bytes 2654212
  34.2 6.4 %collective-permute-start.3 = (f32[64,128]{1,0:T(8,128)S(1)}, f32[64,128]{1,0:T(8,128)S(1)}, u32[]{:S(2)}, u32[]{:S(2)}) collective-permute-start(f32[64,128]{1,0:T(8,128)S(1)} %get-tuple-element.18), channel_id=1, source_target_pairs={{0,20},{1,21},{2,22},{3,23},{4,16},{5,17},{6,18},{7,19},{8,28},{9,... | collective-permute-start | bytes 98312 | tf_op jit(solution)/shard_map/ppermute | solution.py:108
  37.7 24.8 %copy-start.2 = (bf16[768,128]{1,0:T(8,128)(2,1)S(1)}, bf16[768,128]{1,0:T(8,128)(2,1)}, u32[]{:S(2)}) copy-start(bf16[768,128]{1,0:T(8,128)(2,1)} %constant.4.clone.move_ref) | copy-start | bytes 589828
  37.7 4.4 %collective-permute-start.2 = (f32[64,128]{1,0:T(8,128)S(1)}, f32[64,128]{1,0:T(8,128)S(1)}, u32[]{:S(2)}, u32[]{:S(2)}) collective-permute-start(f32[64,128]{1,0:T(8,128)S(1)} %get-tuple-element.17.own_ref), channel_id=1, source_target_pairs={{0,4},{1,5},{2,6},{3,7},{4,0},{5,1},{6,2},{7,3},{8,12},{9,13},{10,... | collective-permute-start | bytes 98312 | tf_op jit(solution)/shard_map/ppermute | solution.py:98
  39.3 2.8 %collective-permute-start.1 = (f32[64,128]{1,0:T(8,128)S(1)}, f32[64,128]{1,0:T(8,128)S(1)}, u32[]{:S(2)}, u32[]{:S(2)}) collective-permute-start(f32[64,128]{1,0:T(8,128)S(1)} %get-tuple-element.18), channel_id=1, source_target_pairs={{0,16},{16,32},{32,48},{48,64},{64,80},{80,96},{96,112},{112,128},... | collective-permute-start | bytes 98312 | tf_op jit(solution)/shard_map/ppermute | solution.py:94
  40.6 21.9 %collective-permute-start.5 = (bf16[27,64,256]{2,1,0:T(8,128)(2,1)S(1)}, bf16[27,64,256]{2,1,0:T(8,128)(2,1)S(1)}, u32[]{:S(2)}, u32[]{:S(2)}) collective-permute-start(bf16[27,64,256]{2,1,0:T(8,128)(2,1)S(1)} %copy-done), channel_id=1, source_target_pairs={{0,4},{1,5},{2,6},{3,7},{4,0},{5,1},{6,2},{7,3},{8,12},{9,13},{10,... | collective-permute-start | bytes 2654216 | tf_op jit(solution)/shard_map/ppermute | solution.py:98
  42.3 35.6 %copy-start.1 = (bf16[512,512]{1,0:T(8,128)(2,1)S(1)}, bf16[512,512]{1,0:T(8,128)(2,1)}, u32[]{:S(2)}) copy-start(bf16[512,512]{1,0:T(8,128)(2,1)} %constant.5.clone.spread_ref) | copy-start | bytes 1572868
  57.3 5.2 %collective-permute-start.4 = (bf16[8,80,128]{2,1,0:T(8,128)(2,1)S(1)}, bf16[8,80,128]{2,1,0:T(8,128)(2,1)S(1)}, u32[]{:S(2)}, u32[]{:S(2)}) collective-permute-start(bf16[8,80,128]{2,1,0:T(8,128)(2,1)S(1)} %all_to_all.22.here_ref), channel_id=1, source_target_pairs={{0,16},{16,0},{32,48},{48,32},{64,80},{80,64},{96,112},{112,96},{1... | collective-permute-start | bytes 491528 | tf_op jit(solution)/shard_map/ppermute | solution.py:282

commit v7 on v6

--- a/solution.py
+++ b/solution.py
@@ -53,37 +53,53 @@
         copies_ref[i] = places
 
 
-def block_kernel(whole_ref, weight_ref, *rest):
-    *residual, own_ref, later_ref = rest
+def later_kernel(whole_ref, weight_ref, act_ref, middle_ref, later_ref):
     depth = whole_ref.shape[0]
-    outs = own_ref.shape[0]
+    outs = later_ref.shape[0]
     values = whole_ref[...].astype(F32)
     squares = jnp.sum(values * values, axis=0, keepdims=True)
-    scaled = values * lax.rsqrt(squares / depth + EPSILON)
-    act = (scaled / (1.0 + jnp.exp(-scaled))).astype(BF16)
-    product = jnp.dot(weight_ref[...], act, preferred_element_type=F32)
+    half = values * (0.5 * lax.rsqrt(squares / depth + EPSILON))
+    act = (half + half * jnp.tanh(half)).astype(BF16)
+    act_ref[...] = act
+    product = jnp.dot(weight_ref[: 18 * outs], act, preferred_element_type=F32)
     frame = lane_ids()[1]
     oldest = spatial_sum(product, 0, outs)
     middle = spatial_sum(product, 9, outs)
-    newest = spatial_sum(product, 18, outs)
     first = lax.axis_index("tm") == 0
     start = jnp.where(frame == 0, middle + oldest, pltpu.roll(oldest, COLS, 1))
-    own = newest + jnp.where(frame == 1, pltpu.roll(middle, COLS, 1), 0.0)
-    own = own + jnp.where(first, start, 0.0)
-    for ref in residual:
+    own = jnp.where(frame == 1, pltpu.roll(middle, COLS, 1), 0.0)
+    middle_ref[...] = own + jnp.where(first, start, 0.0)
+    later_ref[...] = oldest + jnp.where(frame == 0, pltpu.roll(middle, LANES - COLS, 1), 0.0)
+
+
+def own_kernel(act_ref, weight_ref, *rest):
+    *parts, own_ref = rest
+    outs = own_ref.shape[0]
+    product = jnp.dot(weight_ref[18 * outs :], act_ref[...], preferred_element_type=F32)
+    own = spatial_sum(product, 0, outs)
+    for ref in parts:
         own = ref[...].astype(F32) + own
     own_ref[...] = own
-    later_ref[...] = oldest + jnp.where(frame == 0, pltpu.roll(middle, LANES - COLS, 1), 0.0)
+
+
+def work(limit, flops):
+    return {
+        "compiler_params": pltpu.CompilerParams(vmem_limit_bytes=limit * MIB),
+        "cost_estimate": pl.CostEstimate(flops=flops, bytes_accessed=MIB, transcendentals=0),
+    }
 
 
 def block_conv(whole, weight, outs, *residual):
     shape = jax.ShapeDtypeStruct((outs, LANES), F32)
-    return pl.pallas_call(
-        block_kernel,
-        out_shape=(shape, shape),
-        compiler_params=pltpu.CompilerParams(vmem_limit_bytes=16 * MIB),
-        cost_estimate=pl.CostEstimate(flops=4 * 10**9, bytes_accessed=8 * MIB, transcendentals=0),
-    )(whole, weight, *residual)
+    act, middle, later = pl.pallas_call(
+        later_kernel,
+        out_shape=(jax.ShapeDtypeStruct(whole.shape, BF16), shape, shape),
+        **work(16, 4 * 10**9),
+    )(whole, weight)
+    own = pl.pallas_call(own_kernel, out_shape=shape, **work(16, 2 * 10**9))(
+        act, weight, middle, *residual
+    )
+    return own, later
 
 
 def next_frames(i):
@@ -143,7 +159,7 @@
     }
 
 
-def upsample_kernel(here_ref, there_ref, move_ref, weight_ref, weight_too_ref, out_ref, moved):
+def moved_kernel(here_ref, there_ref, move_ref, moved):
     chips, _, channels = here_ref.shape
     low = lax.axis_index("tm") % 2 == 0
     inner = jnp.where(middle(), 1.0, 0.0).astype(BF16)
@@ -175,6 +191,9 @@
                         moved[k, band, at * LANES : (at + 1) * LANES] = (
                             piece * inner if seam else piece
                         )
+
+
+def upsample_kernel(moved, weight_ref, weight_too_ref, out_ref):
     blocks = []
     for tap in range(27):
         blocks.append(weight_ref[tap])
@@ -283,12 +302,16 @@
 
     outs = conv_upsample.shape[2]
     rows_here = BANDS * BAND
+    moved = pl.pallas_call(
+        moved_kernel,
+        out_shape=jax.ShapeDtypeStruct((9, BANDS, (BAND + 2) * LANES, 2 * channels), BF16),
+        compiler_params=pltpu.CompilerParams(vmem_limit_bytes=16 * MIB),
+    )(frames, frames_too, moves())
     partial = pl.pallas_call(
         upsample_kernel,
         out_shape=jax.ShapeDtypeStruct((rows_here, LANES, outs), BF16),
-        scratch_shapes=[pltpu.VMEM((9, BANDS, (BAND + 2) * LANES, 2 * channels), BF16)],
-        compiler_params=pltpu.CompilerParams(vmem_limit_bytes=32 * MIB),
-    )(frames, frames_too, moves(), conv_upsample, other)
+        compiler_params=pltpu.CompilerParams(vmem_limit_bytes=24 * MIB),
+    )(moved, conv_upsample, other)
     groups = [
         [place * PAIR + c for place in pair for c in range(PAIR)] for pair in ((1, 2), (3, 0))
     ]

time: 79.4 us -> 79.2 us (level)
  waiting for transfers between devices: 3.37 us -> 1.86 us
  Pallas kernels: 6.67 us -> 7.49 us
    pallas_call x2 -> x5, Pallas kernels: 2.85 us -> 4.19 us  [the longest x2 2.29 us: block_conv(): pl.pallas_call(later_kernel, out_shape=(jax.ShapeDtypeStruct(whole.shape,...]
    ppermute x1, waiting for transfers between devices: 1.31 us -> 0.42 us  [shifted_and_swapped(): return lax.ppermute(later, ('tm', 'chan'), pairs)]
  transfers between devices with their start and end apart: 6 -> 6, of which waited for: 3 -> 3; matrix products, arithmetic and copies ran while one was open for 0% -> 0% of each run, Pallas kernels for 0% -> 3%
where the time goes in v7:
time: 79.2 us; the launch traced here: 78.7 us
  blocking collectives  54 us (68%)
  starting transfers between devices  14.5 us (18%)
  Pallas kernels  7.49 us (9%)
  waiting for transfers between devices  1.86 us (2%)
  local copies, waits for them, and re-layouts  0.8 us (1%)
    all_to_all x2, blocking collectives, on_device(): whole = lax.all_to_all(copies, 'chan', 0, 0, tiled=True).reshape(-1, LANES)  25.7 us
    all_to_all x1, blocking collectives, on_device(): lax.all_to_all(copies, 'tm', 0, 0, tiled=True, axis_index_groups=along)  15.6 us
    all_to_all x1, blocking collectives, on_device(): lax.all_to_all(partial, 'chan', 0, 0, tiled=True, axis_index_groups=groups)  12.7 us
    ppermute x1, starting transfers between devices, on_device(): lax.ppermute(frames, 'tm', [(i, i ^ 1) for i in range(frames_on)])  4.4 us
    ppermute x2, starting transfers between devices, shifted_on(): lax.ppermute(later, 'tm', [(i, next_frames(i)) for i in range(lax.axis_si...  3.56 us
    ppermute x1, starting transfers between devices, shifted_and_swapped(): return lax.ppermute(later, ('tm', 'chan'), pairs)  3.39 us
    ppermute x2, starting transfers between devices, swapped(): lax.ppermute(value, 'chan', [(c, c ^ PAIR) for c in range(lax.axis_size('...  3.1 us
    pallas_call x2, Pallas kernels, block_conv(): pl.pallas_call(later_kernel, out_shape=(jax.ShapeDtypeStruct(whole.shape,...  2.29 us
  transfers between devices with their start and end apart: 6, of which 3 were waited for; matrix products, arithmetic and copies ran while one was open for 0% of the time, Pallas kernels for 3%

profile of v7, /device:TPU:1, one launch (start us, length us, event | category | flops | bytes accessed | tf_op | source)
XLA Modules:
  0.0 78.7 jit_solution(9260959591237507145)
XLA Ops:
  0.0 0.8 copy.7
  0.8 0.1 shard_map.64
  0.9 15.1 %all_to_all.20 = bf16[16,64,128]{2,1,0:T(8,128)(2,1)S(1)} all-to-all(bf16[16,64,128]{2,1,0:T(8,128)(2,1)S(1)} %get-tuple-element.15), channel_id=1, replica_groups=mesh['tm'=16,'chan'=16] {'chan'}, dimensions={0} | all-to-all | bytes 524288 | tf_op jit(solution)/shard_map/all_to_all | solution.py:279
  16.0 1.1 %shard_map.65 = (bf16[1024,128]{1,0:T(8,128)(2,1)S(1)}, f32[64,128]{1,0:T(8,128)S(1)}, f32[64,128]{1,0:T(8,128)S(1)}) custom-call(bf16[1024,128]{1,0:T(8,128)(2,1)S(1)} %bitcast.10, bf16[1728,1024]{1,0:T(8,128)(2,1)S(1)} %bitcast.13), custom_call_target="tpu_custom_call" | custom-call | flops 4000000000 | bytes 1048576 | tf_op jit(solution)/shard_map/pallas_call | solution.py:94
  17.1 3.6 %collective-permute-start = (f32[64,128]{1,0:T(8,128)S(1)}, f32[64,128]{1,0:T(8,128)S(1)}, u32[]{:S(2)}, u32[]{:S(2)}) collective-permute-start(f32[64,128]{1,0:T(8,128)S(1)} %get-tuple-element.18), channel_id=1, source_target_pairs={{0,16},{16,32},{32,48},{48,64},{64,80},{80,96},{96,112},{112,128},... | collective-permute-start | bytes 98312 | tf_op jit(solution)/shard_map/ppermute | solution.py:110
  20.7 0.6 shard_map.66.own_ref
  21.3 0.4 collective-permute-done.earlier_ref
  21.8 10.6 %all_to_all.21 = bf16[16,64,128]{2,1,0:T(8,128)(2,1)S(1)} all-to-all(bf16[16,64,128]{2,1,0:T(8,128)(2,1)S(1)} %shard_map.67), channel_id=1, replica_groups=mesh['tm'=16,'chan'=16] {'chan'}, dimensions={0} | all-to-all | bytes 524288 | tf_op jit(solution)/shard_map/all_to_all | solution.py:285
  32.4 1.1 %shard_map.68 = (bf16[1024,128]{1,0:T(8,128)(2,1)S(1)}, f32[64,128]{1,0:T(8,128)S(1)}, f32[64,128]{1,0:T(8,128)S(1)}) custom-call(bf16[1024,128]{1,0:T(8,128)(2,1)S(1)} %bitcast.11, bf16[1728,1024]{1,0:T(8,128)(2,1)S(1)} %bitcast.15), custom_call_target="tpu_custom_call" | custom-call | flops 4000000000 | bytes 1048576 | tf_op jit(solution)/shard_map/pallas_call | solution.py:94
  33.5 3.4 %collective-permute-start.3 = (f32[64,128]{1,0:T(8,128)S(1)}, f32[64,128]{1,0:T(8,128)S(1)}, u32[]{:S(2)}, u32[]{:S(2)}) collective-permute-start(f32[64,128]{1,0:T(8,128)S(1)} %get-tuple-element.22), channel_id=1, source_target_pairs={{0,20},{1,21},{2,22},{3,23},{4,16},{5,17},{6,18},{7,19},{8,28},{9,... | collective-permute-start | bytes 98312 | tf_op jit(solution)/shard_map/ppermute | solution.py:124
  36.9 0.6 shard_map.69.own_ref
  37.5 0.0 copy-start.2
  37.5 1.6 %collective-permute-start.2 = (f32[64,128]{1,0:T(8,128)S(1)}, f32[64,128]{1,0:T(8,128)S(1)}, u32[]{:S(2)}, u32[]{:S(2)}) collective-permute-start(f32[64,128]{1,0:T(8,128)S(1)} %shard_map.69.own_ref), channel_id=1, source_target_pairs={{0,4},{1,5},{2,6},{3,7},{4,0},{5,1},{6,2},{7,3},{8,12},{9,13},{10,... | collective-permute-start | bytes 98312 | tf_op jit(solution)/shard_map/ppermute | solution.py:114
  39.2 0.4 collective-permute-done.3.earlier_too_ref
  39.6 1.5 %collective-permute-start.5 = (bf16[27,64,256]{2,1,0:T(8,128)(2,1)S(1)}, bf16[27,64,256]{2,1,0:T(8,128)(2,1)S(1)}, u32[]{:S(2)}, u32[]{:S(2)}) collective-permute-start(bf16[27,64,256]{2,1,0:T(8,128)(2,1)S(1)} %copy-done), channel_id=1, source_target_pairs={{0,4},{1,5},{2,6},{3,7},{4,0},{5,1},{6,2},{7,3},{8,12},{9,13},{10,... | collective-permute-start | bytes 2654216 | tf_op jit(solution)/shard_map/ppermute | solution.py:114
  41.1 0.2 shard_map.70
  41.3 15.6 %all_to_all.22.here_ref = bf16[8,80,128]{2,1,0:T(8,128)(2,1)S(1)} all-to-all(bf16[8,80,128]{2,1,0:T(8,128)(2,1)S(1)} %shard_map.70), channel_id=1, replica_groups={{0,32,64,96,128,160,192,224},{16,48,80,112,144,176,208,240},{1,33,65,97..., dimensions={0} | all-to-all | bytes 327680 | tf_op jit(solution)/shard_map/all_to_all | solution.py:300
  56.8 4.4 %collective-permute-start.4 = (bf16[8,80,128]{2,1,0:T(8,128)(2,1)S(1)}, bf16[8,80,128]{2,1,0:T(8,128)(2,1)S(1)}, u32[]{:S(2)}, u32[]{:S(2)}) collective-permute-start(bf16[8,80,128]{2,1,0:T(8,128)(2,1)S(1)} %all_to_all.22.here_ref), channel_id=1, source_target_pairs={{0,16},{16,0},{32,48},{48,32},{64,80},{80,64},{96,112},{112,96},{1... | collective-permute-start | bytes 491528 | tf_op jit(solution)/shard_map/ppermute | solution.py:301
  61.2 1.0 %collective-permute-done.4.there_ref = bf16[8,80,128]{2,1,0:T(8,128)(2,1)S(1)} collective-permute-done((bf16[8,80,128]{2,1,0:T(8,128)(2,1)S(1)}, bf16[8,80,128]{2,1,0:T(8,128)(2,1)S(1)}, u32[]{:S(2)}, u32[]{:S(2)}) %collective-permute-start.4) | collective-permute-done | bytes 163872 | tf_op jit(solution)/shard_map/ppermute | solution.py:301
  62.3 0.7 shard_map.71.moved
  63.0 0.0 copy-start.1
  63.0 2.1 %shard_map.72 = bf16[8,128,256]{2,1,0:T(8,128)(2,1)S(1)} custom-call(bf16[9,2,768,128]{3,2,1,0:T(8,128)(2,1)S(1)} %shard_map.71.moved, bf16[27,64,256]{2,1,0:T(8,128)(2,1)S(1)} %copy-done, bf16[27,64,256]{2,1,0:T(8,128)(2,1)S(1)} %collective-permute-done.5.weight_too_ref), custom_call_target="tpu_custom_call" | custom-call | tf_op jit(solution)/shard_map/pallas_call | solution.py:310
  65.0 12.7 %all_to_all.23.parts_ref = bf16[8,128,256]{2,1,0:T(8,128)(2,1)S(1)} all-to-all(bf16[8,128,256]{2,1,0:T(8,128)(2,1)S(1)} %shard_map.72), channel_id=1, replica_groups={{4,5,6,7,8,9,10,11},{12,13,14,15,0,1,2,3},{20,21,22,23,24,25,26,27},{28..., dimensions={0} | all-to-all | bytes 1048576 | tf_op jit(solution)/shard_map/all_to_all | solution.py:318
  77.7 1.0 %shard_map.73 = bf16[2,32,512]{2,1,0:T(8,128)(2,1)} custom-call(bf16[8,128,256]{2,1,0:T(8,128)(2,1)S(1)} %all_to_all.23.parts_ref, bf16[512,512]{1,0:T(8,128)(2,1)S(1)} %copy-done.1), custom_call_target="tpu_custom_call" | custom-call | tf_op jit(solution)/shard_map/pallas_call | solution.py:319
  (13 shorter events, 0.1 us)
Async XLA Ops:
  0.8 15.2 %copy-start.3 = (bf16[64,27,1024]{2,0,1:T(8,128)(2,1)S(1)}, bf16[64,27,1024]{2,0,1:T(8,128)(2,1)}, u32[]{:S(2)}) copy-start(bf16[64,27,1024]{2,0,1:T(8,128)(2,1)} %param.7) | copy-start | bytes 10616836
  17.1 4.6 %collective-permute-start = (f32[64,128]{1,0:T(8,128)S(1)}, f32[64,128]{1,0:T(8,128)S(1)}, u32[]{:S(2)}, u32[]{:S(2)}) collective-permute-start(f32[64,128]{1,0:T(8,128)S(1)} %get-tuple-element.18), channel_id=1, source_target_pairs={{0,16},{16,32},{32,48},{48,64},{64,80},{80,96},{96,112},{112,128},... | collective-permute-start | bytes 98312 | tf_op jit(solution)/shard_map/ppermute | solution.py:110
  21.3 11.0 %copy-start.4 = (bf16[64,27,1024]{2,0,1:T(8,128)(2,1)S(1)}, bf16[64,27,1024]{2,0,1:T(8,128)(2,1)}, u32[]{:S(2)}) copy-start(bf16[64,27,1024]{2,0,1:T(8,128)(2,1)} %param.8) | copy-start | bytes 10616836
  33.5 6.1 %collective-permute-start.3 = (f32[64,128]{1,0:T(8,128)S(1)}, f32[64,128]{1,0:T(8,128)S(1)}, u32[]{:S(2)}, u32[]{:S(2)}) collective-permute-start(f32[64,128]{1,0:T(8,128)S(1)} %get-tuple-element.22), channel_id=1, source_target_pairs={{0,20},{1,21},{2,22},{3,23},{4,16},{5,17},{6,18},{7,19},{8,28},{9,... | collective-permute-start | bytes 98312 | tf_op jit(solution)/shard_map/ppermute | solution.py:124
  36.9 2.7 %copy-start = (bf16[27,64,256]{2,1,0:T(8,128)(2,1)S(1)}, bf16[27,64,256]{2,1,0:T(8,128)(2,1)}, u32[]{:S(2)}) copy-start(bf16[27,64,256]{2,1,0:T(8,128)(2,1)} %weight_ref.1) | copy-start | bytes 2654212
  37.5 24.7 %copy-start.2 = (bf16[768,128]{1,0:T(8,128)(2,1)S(1)}, bf16[768,128]{1,0:T(8,128)(2,1)}, u32[]{:S(2)}) copy-start(bf16[768,128]{1,0:T(8,128)(2,1)} %constant.4.clone.move_ref) | copy-start | bytes 589828
  37.5 3.5 %collective-permute-start.2 = (f32[64,128]{1,0:T(8,128)S(1)}, f32[64,128]{1,0:T(8,128)S(1)}, u32[]{:S(2)}, u32[]{:S(2)}) collective-permute-start(f32[64,128]{1,0:T(8,128)S(1)} %shard_map.69.own_ref), channel_id=1, source_target_pairs={{0,4},{1,5},{2,6},{3,7},{4,0},{5,1},{6,2},{7,3},{8,12},{9,13},{10,... | collective-permute-start | bytes 98312 | tf_op jit(solution)/shard_map/ppermute | solution.py:114
  39.1 1.9 %collective-permute-start.1 = (f32[64,128]{1,0:T(8,128)S(1)}, f32[64,128]{1,0:T(8,128)S(1)}, u32[]{:S(2)}, u32[]{:S(2)}) collective-permute-start(f32[64,128]{1,0:T(8,128)S(1)} %get-tuple-element.22), channel_id=1, source_target_pairs={{0,16},{16,32},{32,48},{48,64},{64,80},{80,96},{96,112},{112,128},... | collective-permute-start | bytes 98312 | tf_op jit(solution)/shard_map/ppermute | solution.py:110
  39.6 23.4 %collective-permute-start.5 = (bf16[27,64,256]{2,1,0:T(8,128)(2,1)S(1)}, bf16[27,64,256]{2,1,0:T(8,128)(2,1)S(1)}, u32[]{:S(2)}, u32[]{:S(2)}) collective-permute-start(bf16[27,64,256]{2,1,0:T(8,128)(2,1)S(1)} %copy-done), channel_id=1, source_target_pairs={{0,4},{1,5},{2,6},{3,7},{4,0},{5,1},{6,2},{7,3},{8,12},{9,13},{10,... | collective-permute-start | bytes 2654216 | tf_op jit(solution)/shard_map/ppermute | solution.py:114
  56.8 5.4 %collective-permute-start.4 = (bf16[8,80,128]{2,1,0:T(8,128)(2,1)S(1)}, bf16[8,80,128]{2,1,0:T(8,128)(2,1)S(1)}, u32[]{:S(2)}, u32[]{:S(2)}) collective-permute-start(bf16[8,80,128]{2,1,0:T(8,128)(2,1)S(1)} %all_to_all.22.here_ref), channel_id=1, source_target_pairs={{0,16},{16,0},{32,48},{48,32},{64,80},{80,64},{96,112},{112,96},{1... | collective-permute-start | bytes 491528 | tf_op jit(solution)/shard_map/ppermute | solution.py:301
  63.0 14.8 %copy-start.1 = (bf16[512,512]{1,0:T(8,128)(2,1)S(1)}, bf16[512,512]{1,0:T(8,128)(2,1)}, u32[]{:S(2)}) copy-start(bf16[512,512]{1,0:T(8,128)(2,1)} %constant.5.clone.spread_ref) | copy-start | bytes 1572868

commit v8 on v7

--- a/solution.py
+++ b/solution.py
@@ -58,8 +58,8 @@
     outs = later_ref.shape[0]
     values = whole_ref[...].astype(F32)
     squares = jnp.sum(values * values, axis=0, keepdims=True)
-    half = values * (0.5 * lax.rsqrt(squares / depth + EPSILON))
-    act = (half + half * jnp.tanh(half)).astype(BF16)
+    scaled = values * lax.rsqrt(squares / depth + EPSILON)
+    act = (scaled / (1.0 + jnp.exp(-scaled))).astype(BF16)
     act_ref[...] = act
     product = jnp.dot(weight_ref[: 18 * outs], act, preferred_element_type=F32)
     frame = lane_ids()[1]

time: 79.2 us -> 79.2 us (level)
  no operation moved by 1% of the time
where the time goes in v8:
time: 79.2 us; the launch traced here: 78.8 us
  blocking collectives  54 us (68%)
  starting transfers between devices  14.4 us (18%)
  Pallas kernels  7.56 us (10%)
  waiting for transfers between devices  1.86 us (2%)
  local copies, waits for them, and re-layouts  0.8 us (1%)
    all_to_all x2, blocking collectives, on_device(): whole = lax.all_to_all(copies, 'chan', 0, 0, tiled=True).reshape(-1, LANES)  25.7 us
    all_to_all x1, blocking collectives, on_device(): lax.all_to_all(copies, 'tm', 0, 0, tiled=True, axis_index_groups=along)  15.6 us
    all_to_all x1, blocking collectives, on_device(): lax.all_to_all(partial, 'chan', 0, 0, tiled=True, axis_index_groups=groups)  12.7 us
    ppermute x1, starting transfers between devices, on_device(): lax.ppermute(frames, 'tm', [(i, i ^ 1) for i in range(frames_on)])  4.4 us
    ppermute x2, starting transfers between devices, shifted_on(): lax.ppermute(later, 'tm', [(i, next_frames(i)) for i in range(lax.axis_si...  3.56 us
    ppermute x1, starting transfers between devices, shifted_and_swapped(): return lax.ppermute(later, ('tm', 'chan'), pairs)  3.39 us
    ppermute x2, starting transfers between devices, swapped(): lax.ppermute(value, 'chan', [(c, c ^ PAIR) for c in range(lax.axis_size('...  3.1 us
    pallas_call x2, Pallas kernels, block_conv(): pl.pallas_call(later_kernel, out_shape=(jax.ShapeDtypeStruct(whole.shape,...  2.37 us
  transfers between devices with their start and end apart: 6, of which 3 were waited for; matrix products, arithmetic and copies ran while one was open for 0% of the time, Pallas kernels for 3%

profile of v8, /device:TPU:1, one launch (start us, length us, event | category | flops | bytes accessed | tf_op | source)
XLA Modules:
  0.0 78.8 jit_solution(11155469229179865481)
XLA Ops:
  0.0 0.8 copy.7
  0.8 0.1 shard_map.64
  0.9 15.1 %all_to_all.20 = bf16[16,64,128]{2,1,0:T(8,128)(2,1)S(1)} all-to-all(bf16[16,64,128]{2,1,0:T(8,128)(2,1)S(1)} %get-tuple-element.15), channel_id=1, replica_groups=mesh['tm'=16,'chan'=16] {'chan'}, dimensions={0} | all-to-all | bytes 524288 | tf_op jit(solution)/shard_map/all_to_all | solution.py:279
  16.0 1.2 %shard_map.65 = (bf16[1024,128]{1,0:T(8,128)(2,1)S(1)}, f32[64,128]{1,0:T(8,128)S(1)}, f32[64,128]{1,0:T(8,128)S(1)}) custom-call(bf16[1024,128]{1,0:T(8,128)(2,1)S(1)} %bitcast.10, bf16[1728,1024]{1,0:T(8,128)(2,1)S(1)} %bitcast.13), custom_call_target="tpu_custom_call" | custom-call | flops 4000000000 | bytes 1048576 | tf_op jit(solution)/shard_map/pallas_call | solution.py:94
  17.2 3.6 %collective-permute-start = (f32[64,128]{1,0:T(8,128)S(1)}, f32[64,128]{1,0:T(8,128)S(1)}, u32[]{:S(2)}, u32[]{:S(2)}) collective-permute-start(f32[64,128]{1,0:T(8,128)S(1)} %get-tuple-element.18), channel_id=1, source_target_pairs={{0,16},{16,32},{32,48},{48,64},{64,80},{80,96},{96,112},{112,128},... | collective-permute-start | bytes 98312 | tf_op jit(solution)/shard_map/ppermute | solution.py:110
  20.7 0.6 shard_map.66.own_ref
  21.4 0.4 collective-permute-done.earlier_ref
  21.8 10.6 %all_to_all.21 = bf16[16,64,128]{2,1,0:T(8,128)(2,1)S(1)} all-to-all(bf16[16,64,128]{2,1,0:T(8,128)(2,1)S(1)} %shard_map.67), channel_id=1, replica_groups=mesh['tm'=16,'chan'=16] {'chan'}, dimensions={0} | all-to-all | bytes 524288 | tf_op jit(solution)/shard_map/all_to_all | solution.py:285
  32.4 1.2 %shard_map.68 = (bf16[1024,128]{1,0:T(8,128)(2,1)S(1)}, f32[64,128]{1,0:T(8,128)S(1)}, f32[64,128]{1,0:T(8,128)S(1)}) custom-call(bf16[1024,128]{1,0:T(8,128)(2,1)S(1)} %bitcast.11, bf16[1728,1024]{1,0:T(8,128)(2,1)S(1)} %bitcast.15), custom_call_target="tpu_custom_call" | custom-call | flops 4000000000 | bytes 1048576 | tf_op jit(solution)/shard_map/pallas_call | solution.py:94
  33.6 3.4 %collective-permute-start.3 = (f32[64,128]{1,0:T(8,128)S(1)}, f32[64,128]{1,0:T(8,128)S(1)}, u32[]{:S(2)}, u32[]{:S(2)}) collective-permute-start(f32[64,128]{1,0:T(8,128)S(1)} %get-tuple-element.22), channel_id=1, source_target_pairs={{0,20},{1,21},{2,22},{3,23},{4,16},{5,17},{6,18},{7,19},{8,28},{9,... | collective-permute-start | bytes 98312 | tf_op jit(solution)/shard_map/ppermute | solution.py:124
  37.0 0.6 shard_map.69.own_ref
  37.6 0.0 copy-start.2
  37.6 1.6 %collective-permute-start.2 = (f32[64,128]{1,0:T(8,128)S(1)}, f32[64,128]{1,0:T(8,128)S(1)}, u32[]{:S(2)}, u32[]{:S(2)}) collective-permute-start(f32[64,128]{1,0:T(8,128)S(1)} %shard_map.69.own_ref), channel_id=1, source_target_pairs={{0,4},{1,5},{2,6},{3,7},{4,0},{5,1},{6,2},{7,3},{8,12},{9,13},{10,... | collective-permute-start | bytes 98312 | tf_op jit(solution)/shard_map/ppermute | solution.py:114
  39.2 0.4 collective-permute-done.3.earlier_too_ref
  39.6 1.5 %collective-permute-start.5 = (bf16[27,64,256]{2,1,0:T(8,128)(2,1)S(1)}, bf16[27,64,256]{2,1,0:T(8,128)(2,1)S(1)}, u32[]{:S(2)}, u32[]{:S(2)}) collective-permute-start(bf16[27,64,256]{2,1,0:T(8,128)(2,1)S(1)} %copy-done), channel_id=1, source_target_pairs={{0,4},{1,5},{2,6},{3,7},{4,0},{5,1},{6,2},{7,3},{8,12},{9,13},{10,... | collective-permute-start | bytes 2654216 | tf_op jit(solution)/shard_map/ppermute | solution.py:114
  41.1 0.2 shard_map.70
  41.3 15.6 %all_to_all.22.here_ref = bf16[8,80,128]{2,1,0:T(8,128)(2,1)S(1)} all-to-all(bf16[8,80,128]{2,1,0:T(8,128)(2,1)S(1)} %shard_map.70), channel_id=1, replica_groups={{0,32,64,96,128,160,192,224},{16,48,80,112,144,176,208,240},{1,33,65,97..., dimensions={0} | all-to-all | bytes 327680 | tf_op jit(solution)/shard_map/all_to_all | solution.py:300
  56.9 4.4 %collective-permute-start.4 = (bf16[8,80,128]{2,1,0:T(8,128)(2,1)S(1)}, bf16[8,80,128]{2,1,0:T(8,128)(2,1)S(1)}, u32[]{:S(2)}, u32[]{:S(2)}) collective-permute-start(bf16[8,80,128]{2,1,0:T(8,128)(2,1)S(1)} %all_to_all.22.here_ref), channel_id=1, source_target_pairs={{0,16},{16,0},{32,48},{48,32},{64,80},{80,64},{96,112},{112,96},{1... | collective-permute-start | bytes 491528 | tf_op jit(solution)/shard_map/ppermute | solution.py:301
  61.3 1.0 %collective-permute-done.4.there_ref = bf16[8,80,128]{2,1,0:T(8,128)(2,1)S(1)} collective-permute-done((bf16[8,80,128]{2,1,0:T(8,128)(2,1)S(1)}, bf16[8,80,128]{2,1,0:T(8,128)(2,1)S(1)}, u32[]{:S(2)}, u32[]{:S(2)}) %collective-permute-start.4) | collective-permute-done | bytes 163872 | tf_op jit(solution)/shard_map/ppermute | solution.py:301
  62.3 0.7 shard_map.71.moved
  63.0 0.0 copy-start.1
  63.0 2.1 %shard_map.72 = bf16[8,128,256]{2,1,0:T(8,128)(2,1)S(1)} custom-call(bf16[9,2,768,128]{3,2,1,0:T(8,128)(2,1)S(1)} %shard_map.71.moved, bf16[27,64,256]{2,1,0:T(8,128)(2,1)S(1)} %copy-done, bf16[27,64,256]{2,1,0:T(8,128)(2,1)S(1)} %collective-permute-done.5.weight_too_ref), custom_call_target="tpu_custom_call" | custom-call | tf_op jit(solution)/shard_map/pallas_call | solution.py:310
  65.1 12.7 %all_to_all.23.parts_ref = bf16[8,128,256]{2,1,0:T(8,128)(2,1)S(1)} all-to-all(bf16[8,128,256]{2,1,0:T(8,128)(2,1)S(1)} %shard_map.72), channel_id=1, replica_groups={{4,5,6,7,8,9,10,11},{12,13,14,15,0,1,2,3},{20,21,22,23,24,25,26,27},{28..., dimensions={0} | all-to-all | bytes 1048576 | tf_op jit(solution)/shard_map/all_to_all | solution.py:318
  77.8 1.0 %shard_map.73 = bf16[2,32,512]{2,1,0:T(8,128)(2,1)} custom-call(bf16[8,128,256]{2,1,0:T(8,128)(2,1)S(1)} %all_to_all.23.parts_ref, bf16[512,512]{1,0:T(8,128)(2,1)S(1)} %copy-done.1), custom_call_target="tpu_custom_call" | custom-call | tf_op jit(solution)/shard_map/pallas_call | solution.py:319
  (13 shorter events, 0.1 us)
Async XLA Ops:
  0.8 15.2 %copy-start.3 = (bf16[64,27,1024]{2,0,1:T(8,128)(2,1)S(1)}, bf16[64,27,1024]{2,0,1:T(8,128)(2,1)}, u32[]{:S(2)}) copy-start(bf16[64,27,1024]{2,0,1:T(8,128)(2,1)} %param.7) | copy-start | bytes 10616836
  17.2 4.6 %collective-permute-start = (f32[64,128]{1,0:T(8,128)S(1)}, f32[64,128]{1,0:T(8,128)S(1)}, u32[]{:S(2)}, u32[]{:S(2)}) collective-permute-start(f32[64,128]{1,0:T(8,128)S(1)} %get-tuple-element.18), channel_id=1, source_target_pairs={{0,16},{16,32},{32,48},{48,64},{64,80},{80,96},{96,112},{112,128},... | collective-permute-start | bytes 98312 | tf_op jit(solution)/shard_map/ppermute | solution.py:110
  21.3 11.0 %copy-start.4 = (bf16[64,27,1024]{2,0,1:T(8,128)(2,1)S(1)}, bf16[64,27,1024]{2,0,1:T(8,128)(2,1)}, u32[]{:S(2)}) copy-start(bf16[64,27,1024]{2,0,1:T(8,128)(2,1)} %param.8) | copy-start | bytes 10616836
  33.6 6.1 %collective-permute-start.3 = (f32[64,128]{1,0:T(8,128)S(1)}, f32[64,128]{1,0:T(8,128)S(1)}, u32[]{:S(2)}, u32[]{:S(2)}) collective-permute-start(f32[64,128]{1,0:T(8,128)S(1)} %get-tuple-element.22), channel_id=1, source_target_pairs={{0,20},{1,21},{2,22},{3,23},{4,16},{5,17},{6,18},{7,19},{8,28},{9,... | collective-permute-start | bytes 98312 | tf_op jit(solution)/shard_map/ppermute | solution.py:124
  37.0 2.7 %copy-start = (bf16[27,64,256]{2,1,0:T(8,128)(2,1)S(1)}, bf16[27,64,256]{2,1,0:T(8,128)(2,1)}, u32[]{:S(2)}) copy-start(bf16[27,64,256]{2,1,0:T(8,128)(2,1)} %weight_ref.1) | copy-start | bytes 2654212
  37.6 24.7 %copy-start.2 = (bf16[768,128]{1,0:T(8,128)(2,1)S(1)}, bf16[768,128]{1,0:T(8,128)(2,1)}, u32[]{:S(2)}) copy-start(bf16[768,128]{1,0:T(8,128)(2,1)} %constant.4.clone.move_ref) | copy-start | bytes 589828
  37.6 3.5 %collective-permute-start.2 = (f32[64,128]{1,0:T(8,128)S(1)}, f32[64,128]{1,0:T(8,128)S(1)}, u32[]{:S(2)}, u32[]{:S(2)}) collective-permute-start(f32[64,128]{1,0:T(8,128)S(1)} %shard_map.69.own_ref), channel_id=1, source_target_pairs={{0,4},{1,5},{2,6},{3,7},{4,0},{5,1},{6,2},{7,3},{8,12},{9,13},{10,... | collective-permute-start | bytes 98312 | tf_op jit(solution)/shard_map/ppermute | solution.py:114
  39.2 1.9 %collective-permute-start.1 = (f32[64,128]{1,0:T(8,128)S(1)}, f32[64,128]{1,0:T(8,128)S(1)}, u32[]{:S(2)}, u32[]{:S(2)}) collective-permute-start(f32[64,128]{1,0:T(8,128)S(1)} %get-tuple-element.22), channel_id=1, source_target_pairs={{0,16},{16,32},{32,48},{48,64},{64,80},{80,96},{96,112},{112,128},... | collective-permute-start | bytes 98312 | tf_op jit(solution)/shard_map/ppermute | solution.py:110
  39.6 23.4 %collective-permute-start.5 = (bf16[27,64,256]{2,1,0:T(8,128)(2,1)S(1)}, bf16[27,64,256]{2,1,0:T(8,128)(2,1)S(1)}, u32[]{:S(2)}, u32[]{:S(2)}) collective-permute-start(bf16[27,64,256]{2,1,0:T(8,128)(2,1)S(1)} %copy-done), channel_id=1, source_target_pairs={{0,4},{1,5},{2,6},{3,7},{4,0},{5,1},{6,2},{7,3},{8,12},{9,13},{10,... | collective-permute-start | bytes 2654216 | tf_op jit(solution)/shard_map/ppermute | solution.py:114
  56.9 5.4 %collective-permute-start.4 = (bf16[8,80,128]{2,1,0:T(8,128)(2,1)S(1)}, bf16[8,80,128]{2,1,0:T(8,128)(2,1)S(1)}, u32[]{:S(2)}, u32[]{:S(2)}) collective-permute-start(bf16[8,80,128]{2,1,0:T(8,128)(2,1)S(1)} %all_to_all.22.here_ref), channel_id=1, source_target_pairs={{0,16},{16,0},{32,48},{48,32},{64,80},{80,64},{96,112},{112,96},{1... | collective-permute-start | bytes 491528 | tf_op jit(solution)/shard_map/ppermute | solution.py:301
  63.0 14.8 %copy-start.1 = (bf16[512,512]{1,0:T(8,128)(2,1)S(1)}, bf16[512,512]{1,0:T(8,128)(2,1)}, u32[]{:S(2)}) copy-start(bf16[512,512]{1,0:T(8,128)(2,1)} %constant.5.clone.spread_ref) | copy-start | bytes 1572868
